TPU v7x, 256 devices: a whole 4x4x8 slice. The times are simulated.
256 devices in a mesh: dp: 8 (over z), tensor: 8 (over y, x_hi), seq: 4 (over x_lo, core).
Axes of the slice: x: 4 (x_hi: 2, x_lo: 2; x = x_hi * 2 + x_lo), y: 4, z: 8, core: 2. Of those that a mesh axis runs over, the one named last changes fastest.
Arguments:
- train_act: bfloat16 [8, 4096, 8192], P('dp', 'seq', 'tensor'), may hold values from -0.796875 to 0.796875
- train_grad: bfloat16 [8, 4096, 28672], P('dp', 'seq', 'tensor'), may hold values from -0.59765625 to 0.59765625
- val_act: bfloat16 [1024, 8192], P('dp', 'tensor'), may hold values from -0.796875 to 0.796875
- val_grad: bfloat16 [1024, 28672], P('dp', 'tensor'), may hold values from -0.59765625 to 0.59765625
- val_mask: int32 [1024], P('dp'), may hold values 0 or 1
- lengths: int32 [8], P('dp'), may hold values from 1024 to 4096
Outputs:
- token_values: float32 [8, 4096], P('dp', 'seq')
- example_values: float32 [8], P('dp')
All inputs are finite; a program needn't handle non-finite values. No bound on the sum of `val_mask` on one device may be relied on, other than what follows from the above.
Results may differ from a plain program's by a relative error of at most 0.0003.
Values may be sent and summed in bfloat16 or wider, within the bound.
No kernel may reach another device: no remote copies, remote signals or barrier semaphores. Data moves between devices by JAX's collectives and lax.ppermute only.
A program may use at most 128 MiB of HBM per device.

v0:
```python
import jax
import jax.numpy as jnp
from jax import lax
from jax.sharding import PartitionSpec as P


def from_behind(value, axis, steps):
    count = lax.axis_size(axis)
    pairs = [(source, (source + steps) % count) for source in range(count)]
    return lax.ppermute(value, axis, pairs)


def contract(left, right):
    return lax.dot_general(
        left, right, (((1,), (1,)), ((), ())), preferred_element_type=jnp.float32
    )


def per_device(train_act, train_grad, val_act, val_grad, val_mask, lengths):
    seq_dev, piece, _ = train_act.shape
    rows = seq_dev * piece
    act_rows = train_act.reshape(rows, train_act.shape[2])
    grad_rows = train_grad.reshape(rows, train_grad.shape[2])
    scale = float(val_act.shape[0] * lax.axis_size("dp")) ** (-0.5)
    own_block = (val_act, val_grad, val_mask.astype(jnp.bfloat16))

    def block_terms(block):
        block_act, block_grad, block_mask = block
        act_gram = contract(act_rows, block_act)
        grad_gram = contract(grad_rows, block_grad)
        weights = block_mask.astype(jnp.float32)[None, :]
        act_share, grad_share = (
            lax.psum_scatter(act_gram, "tensor", scatter_dimension=0, tiled=True),
            lax.psum_scatter(grad_gram, "tensor", scatter_dimension=0, tiled=True),
        )
        return jnp.sum(act_share * grad_share * weights, axis=1)

    count = lax.axis_size("dp")
    totals = block_terms(own_block)
    moving = own_block
    for step in range(count - 1):
        moving = from_behind((moving[0], moving[1], moving[2]), "dp", 1)
        totals = totals + block_terms(moving)
    totals = lax.all_gather(totals, "tensor", axis=0, tiled=True)
    positions = lax.axis_index("seq") * piece + jnp.arange(piece)
    live = positions[None, :] < lengths[:, None]
    values = totals.reshape(seq_dev, piece) * scale
    token_values = jnp.where(live, values, jnp.zeros_like(values))
    partial_sums = jnp.sum(token_values, axis=1)
    example_values = lax.psum(partial_sums, "seq") / jnp.sqrt(lengths.astype(jnp.float32))
    return (token_values, example_values)


def solution(mesh):
    return jax.shard_map(
        per_device,
        mesh=mesh,
        in_specs=(
            P("dp", "seq", "tensor"),
            P("dp", "seq", "tensor"),
            P("dp", "tensor"),
            P("dp", "tensor"),
            P("dp"),
            P("dp"),
        ),
        out_specs=(P("dp", "seq"), P("dp")),
        check_vma=False,
    )
```

profile of v0, /device:TPU:1, one launch (start us, length us, event | category | flops | bytes accessed | tf_op | source)
XLA Modules:
  0.0 1306.2 jit_solution(11671408552531904180)
XLA Ops:
  7.2 1.5 copy-done
  8.8 2.5 fusion.30
  11.3 6.2 fusion.14
  17.5 2.5 collective-permute-start
  20.1 1.6 collective-permute-start.1
  21.7 8.3 collective-permute-done
  30.1 1.5 fusion.28
  31.6 18.2 %collective-permute-done.1 = bf16[128,3584]{1,0:T(8,128)(2,1)} collective-permute-done((bf16[128,3584]{1,0:T(8,128)(2,1)S(1)}, bf16[128,3584]{1,0:T(8,128)(2,1)}, u32[]{:S(2)}, u32[]{:S(2)}) %collective-permute-start.1) | collective-permute-done | bytes 917536 | tf_op jit(solution)/shard_map/ppermute | solution.py:10
  49.8 6.1 fusion.12
  56.2 7.7 collective-permute-done.3
  63.9 1.5 fusion.26
  65.5 18.0 %collective-permute-done.4 = bf16[128,3584]{1,0:T(8,128)(2,1)S(1)} collective-permute-done((bf16[128,3584]{1,0:T(8,128)(2,1)}, bf16[128,3584]{1,0:T(8,128)(2,1)S(1)}, u32[]{:S(2)}, u32[]{:S(2)}) %collective-permute-start.4) | collective-permute-done | bytes 917536 | tf_op jit(solution)/shard_map/ppermute | solution.py:10
  83.5 5.9 fusion.10
  89.7 6.7 collective-permute-done.6
  96.3 1.5 fusion.24
  97.9 18.2 %collective-permute-done.7 = bf16[128,3584]{1,0:T(8,128)(2,1)} collective-permute-done((bf16[128,3584]{1,0:T(8,128)(2,1)S(1)}, bf16[128,3584]{1,0:T(8,128)(2,1)}, u32[]{:S(2)}, u32[]{:S(2)}) %collective-permute-start.7) | collective-permute-done | bytes 917536 | tf_op jit(solution)/shard_map/ppermute | solution.py:10
  116.1 6.2 fusion.8
  122.7 6.4 collective-permute-done.9
  129.2 1.5 fusion.22
  130.7 17.3 %collective-permute-done.10 = bf16[128,3584]{1,0:T(8,128)(2,1)S(1)} collective-permute-done((bf16[128,3584]{1,0:T(8,128)(2,1)}, bf16[128,3584]{1,0:T(8,128)(2,1)S(1)}, u32[]{:S(2)}, u32[]{:S(2)}) %collective-permute-start.10) | collective-permute-done | bytes 917536 | tf_op jit(solution)/shard_map/ppermute | solution.py:10
  148.0 5.9 fusion.6
  154.2 6.7 collective-permute-done.12
  160.9 1.5 fusion.20
  162.5 16.3 %collective-permute-done.13 = bf16[128,3584]{1,0:T(8,128)(2,1)} collective-permute-done((bf16[128,3584]{1,0:T(8,128)(2,1)S(1)}, bf16[128,3584]{1,0:T(8,128)(2,1)}, u32[]{:S(2)}, u32[]{:S(2)}) %collective-permute-start.13) | collective-permute-done | bytes 917536 | tf_op jit(solution)/shard_map/ppermute | solution.py:10
  178.8 6.1 fusion.4
  185.2 6.3 collective-permute-done.15
  191.5 1.5 fusion.18
  193.1 15.6 %collective-permute-done.16 = bf16[128,3584]{1,0:T(8,128)(2,1)S(1)} collective-permute-done((bf16[128,3584]{1,0:T(8,128)(2,1)}, bf16[128,3584]{1,0:T(8,128)(2,1)S(1)}, u32[]{:S(2)}, u32[]{:S(2)}) %collective-permute-start.16) | collective-permute-done | bytes 917536 | tf_op jit(solution)/shard_map/ppermute | solution.py:10
  208.7 6.0 fusion.2
  215.0 6.3 collective-permute-done.18
  221.4 1.5 fusion.16
  222.9 14.8 %collective-permute-done.19 = bf16[128,3584]{1,0:T(8,128)(2,1)} collective-permute-done((bf16[128,3584]{1,0:T(8,128)(2,1)S(1)}, bf16[128,3584]{1,0:T(8,128)(2,1)}, u32[]{:S(2)}, u32[]{:S(2)}) %collective-permute-start.19) | collective-permute-done | bytes 917536 | tf_op jit(solution)/shard_map/ppermute | solution.py:10
  237.7 6.2 fusion
  244.1 3.7 collective-permute-done.2
  247.8 3.6 collective-permute-done.5
  251.4 3.6 collective-permute-done.8
  255.0 3.6 collective-permute-done.11
  259.2 2.9 collective-permute-done.14
  262.2 3.5 collective-permute-done.17
  265.8 3.6 collective-permute-done.20
  269.4 1.0 multiply_reduce_fusion.7
  270.4 54.7 %reduce-scatter.23.cloned.1.call-done = f32[128,128]{1,0:T(8,128)} async-done(((f32[1024,128]{1,0:T(8,128)}), f32[128,128]{1,0:T(8,128)}) %reduce-scatter.23.cloned.1.call-update) | async-done | bytes 65552 | tf_op jit(solution)/shard_map/reduce_scatter | solution.py:34
  325.1 1.0 multiply_reduce_fusion.6
  326.1 77.2 %reduce-scatter.25.cloned.1.call-done = f32[128,128]{1,0:T(8,128)} async-done(((f32[1024,128]{1,0:T(8,128)}), f32[128,128]{1,0:T(8,128)}) %reduce-scatter.25.cloned.1.call-update) | async-done | bytes 65552 | tf_op jit(solution)/shard_map/reduce_scatter | solution.py:33
  403.3 78.7 %reduce-scatter.27.cloned.1.call-done = f32[128,128]{1,0:T(8,128)} async-done(((f32[1024,128]{1,0:T(8,128)}), f32[128,128]{1,0:T(8,128)}) %reduce-scatter.27.cloned.1.call-update) | async-done | bytes 65552 | tf_op jit(solution)/shard_map/reduce_scatter | solution.py:34
  482.0 1.0 multiply_reduce_fusion.5
  483.0 77.4 %reduce-scatter.29.cloned.1.call-done = f32[128,128]{1,0:T(8,128)} async-done(((f32[1024,128]{1,0:T(8,128)}), f32[128,128]{1,0:T(8,128)}) %reduce-scatter.29.cloned.1.call-update) | async-done | bytes 65552 | tf_op jit(solution)/shard_map/reduce_scatter | solution.py:33
  560.3 78.8 %reduce-scatter.31.cloned.1.call-done = f32[128,128]{1,0:T(8,128)} async-done(((f32[1024,128]{1,0:T(8,128)}), f32[128,128]{1,0:T(8,128)}) %reduce-scatter.31.cloned.1.call-update) | async-done | bytes 65552 | tf_op jit(solution)/shard_map/reduce_scatter | solution.py:34
  639.2 1.0 multiply_reduce_fusion.4
  640.2 77.4 %reduce-scatter.33.cloned.1.call-done = f32[128,128]{1,0:T(8,128)} async-done(((f32[1024,128]{1,0:T(8,128)}), f32[128,128]{1,0:T(8,128)}) %reduce-scatter.33.cloned.1.call-update) | async-done | bytes 65552 | tf_op jit(solution)/shard_map/reduce_scatter | solution.py:33
  717.5 78.7 %reduce-scatter.35.cloned.1.call-done = f32[128,128]{1,0:T(8,128)} async-done(((f32[1024,128]{1,0:T(8,128)}), f32[128,128]{1,0:T(8,128)}) %reduce-scatter.35.cloned.1.call-update) | async-done | bytes 65552 | tf_op jit(solution)/shard_map/reduce_scatter | solution.py:34
  796.2 1.0 multiply_reduce_fusion.3
  797.2 77.4 %reduce-scatter.37.cloned.1.call-done = f32[128,128]{1,0:T(8,128)} async-done(((f32[1024,128]{1,0:T(8,128)}), f32[128,128]{1,0:T(8,128)}) %reduce-scatter.37.cloned.1.call-update) | async-done | bytes 65552 | tf_op jit(solution)/shard_map/reduce_scatter | solution.py:33
  874.6 78.7 %reduce-scatter.39.cloned.1.call-done = f32[128,128]{1,0:T(8,128)} async-done(((f32[1024,128]{1,0:T(8,128)}), f32[128,128]{1,0:T(8,128)}) %reduce-scatter.39.cloned.1.call-update) | async-done | bytes 65552 | tf_op jit(solution)/shard_map/reduce_scatter | solution.py:34
  953.3 1.0 multiply_reduce_fusion.2
  954.2 77.4 %reduce-scatter.41.cloned.1.call-done = f32[128,128]{1,0:T(8,128)} async-done(((f32[1024,128]{1,0:T(8,128)}), f32[128,128]{1,0:T(8,128)}) %reduce-scatter.41.cloned.1.call-update) | async-done | bytes 65552 | tf_op jit(solution)/shard_map/reduce_scatter | solution.py:33
  1031.6 78.6 %reduce-scatter.43.cloned.1.call-done = f32[128,128]{1,0:T(8,128)} async-done(((f32[1024,128]{1,0:T(8,128)}), f32[128,128]{1,0:T(8,128)}) %reduce-scatter.43.cloned.1.call-update) | async-done | bytes 65552 | tf_op jit(solution)/shard_map/reduce_scatter | solution.py:34
  1110.2 1.0 multiply_reduce_fusion.1
  1111.2 77.2 %reduce-scatter.45.cloned.1.call-done = f32[128,128]{1,0:T(8,128)} async-done(((f32[1024,128]{1,0:T(8,128)}), f32[128,128]{1,0:T(8,128)}) %reduce-scatter.45.cloned.1.call-update) | async-done | bytes 65552 | tf_op jit(solution)/shard_map/reduce_scatter | solution.py:33
  1188.4 78.5 %reduce-scatter.47.cloned.1.call-done = f32[128,128]{1,0:T(8,128)} async-done(((f32[1024,128]{1,0:T(8,128)}), f32[128,128]{1,0:T(8,128)}) %reduce-scatter.47.cloned.1.call-update) | async-done | bytes 65552 | tf_op jit(solution)/shard_map/reduce_scatter | solution.py:34
  1266.9 1.0 multiply_reduce_fusion
  1267.9 16.9 %all-gather = f32[8,1,128]{2,1,0:T(1,128)S(1)} all-gather(f32[1,1,128]{2,1,0:T(1,128)S(1)} %add_bitcast_fusion), channel_id=1, replica_groups=mesh['dp'=8,'tensor'=8,'seq'=4] {'tensor'}, dimensions={0}, use_global_device_ids=true | all-gather | bytes 4608 | tf_op jit(solution)/shard_map/all_gather | solution.py:44
  1284.7 1.3 fusion.33
  1286.0 11.9 psum.7
  (71 shorter events, 2.3 us)
Async XLA Ops:
  7.2 1.6 copy-start
  7.2 10.4 copy-start.1
  7.2 12.9 copy-start.2
  7.2 262.2 %reduce-scatter.17.cloned.1.call-start = ((), (), s32[]{:S(2)}) async-start(), calls=%async_computation.16 | async-start | bytes 589824 | tf_op jit(solution)/shard_map/reduce_scatter | solution.py:33
  11.2 258.2 %reduce-scatter.19.cloned.1.call-start = ((), (), s32[]{:S(2)}) async-start(), calls=%async_computation.17 | async-start | bytes 589824 | tf_op jit(solution)/shard_map/reduce_scatter | solution.py:34
  17.5 252.9 %reduce-scatter.21.cloned.1.call-start = ((), (), s32[]{:S(2)}) async-start(), calls=%async_computation.18 | async-start | bytes 589824 | tf_op jit(solution)/shard_map/reduce_scatter | solution.py:33
  17.5 12.5 collective-permute-start
  20.1 29.7 %collective-permute-start.1 = (bf16[128,3584]{1,0:T(8,128)(2,1)S(1)}, bf16[128,3584]{1,0:T(8,128)(2,1)}, u32[]{:S(2)}, u32[]{:S(2)}) collective-permute-start(bf16[128,3584]{1,0:T(8,128)(2,1)S(1)} %copy-done.2), channel_id=1, source_target_pairs={{0,32},{32,64},{64,96},{96,128},{128,160},{160,192},{192,224},{224... | collective-permute-start | bytes 2752520 | tf_op jit(solution)/shard_map/ppermute | solution.py:10
  31.6 293.5 %reduce-scatter.23.cloned.1.call-start = ((), (), s32[]{:S(2)}) async-start(), calls=%async_computation.19 | async-start | bytes 589824 | tf_op jit(solution)/shard_map/reduce_scatter | solution.py:34
  56.0 347.4 %reduce-scatter.25.cloned.1.call-start = ((), (), s32[]{:S(2)}) async-start(), calls=%async_computation.20 | async-start | bytes 589824 | tf_op jit(solution)/shard_map/reduce_scatter | solution.py:33
  56.0 7.9 collective-permute-start.3
  56.1 27.4 %collective-permute-start.4 = (bf16[128,3584]{1,0:T(8,128)(2,1)}, bf16[128,3584]{1,0:T(8,128)(2,1)S(1)}, u32[]{:S(2)}, u32[]{:S(2)}) collective-permute-start(bf16[128,3584]{1,0:T(8,128)(2,1)} %collective-permute-done.1), channel_id=1, source_target_pairs={{0,32},{32,64},{64,96},{96,128},{128,160},{160,192},{192,224},{224... | collective-permute-start | bytes 2752520 | tf_op jit(solution)/shard_map/ppermute | solution.py:10
  65.4 416.5 %reduce-scatter.27.cloned.1.call-start = ((), (), s32[]{:S(2)}) async-start(), calls=%async_computation.21 | async-start | bytes 589824 | tf_op jit(solution)/shard_map/reduce_scatter | solution.py:34
  89.4 470.9 %reduce-scatter.29.cloned.1.call-start = ((), (), s32[]{:S(2)}) async-start(), calls=%async_computation.22 | async-start | bytes 589824 | tf_op jit(solution)/shard_map/reduce_scatter | solution.py:33
  89.5 6.9 collective-permute-start.6
  89.6 26.5 %collective-permute-start.7 = (bf16[128,3584]{1,0:T(8,128)(2,1)S(1)}, bf16[128,3584]{1,0:T(8,128)(2,1)}, u32[]{:S(2)}, u32[]{:S(2)}) collective-permute-start(bf16[128,3584]{1,0:T(8,128)(2,1)S(1)} %collective-permute-done.4), channel_id=1, source_target_pairs={{0,32},{32,64},{64,96},{96,128},{128,160},{160,192},{192,224},{224... | collective-permute-start | bytes 2752520 | tf_op jit(solution)/shard_map/ppermute | solution.py:10
  97.9 541.3 %reduce-scatter.31.cloned.1.call-start = ((), (), s32[]{:S(2)}) async-start(), calls=%async_computation.23 | async-start | bytes 589824 | tf_op jit(solution)/shard_map/reduce_scatter | solution.py:34
  122.3 595.2 %reduce-scatter.33.cloned.1.call-start = ((), (), s32[]{:S(2)}) async-start(), calls=%async_computation.24 | async-start | bytes 589824 | tf_op jit(solution)/shard_map/reduce_scatter | solution.py:33
  122.4 6.8 collective-permute-start.9
  122.5 25.5 %collective-permute-start.10 = (bf16[128,3584]{1,0:T(8,128)(2,1)}, bf16[128,3584]{1,0:T(8,128)(2,1)S(1)}, u32[]{:S(2)}, u32[]{:S(2)}) collective-permute-start(bf16[128,3584]{1,0:T(8,128)(2,1)} %collective-permute-done.7), channel_id=1, source_target_pairs={{0,32},{32,64},{64,96},{96,128},{128,160},{160,192},{192,224},{224... | collective-permute-start | bytes 2752520 | tf_op jit(solution)/shard_map/ppermute | solution.py:10
  130.7 665.5 %reduce-scatter.35.cloned.1.call-start = ((), (), s32[]{:S(2)}) async-start(), calls=%async_computation.25 | async-start | bytes 589824 | tf_op jit(solution)/shard_map/reduce_scatter | solution.py:34
  154.0 720.6 %reduce-scatter.37.cloned.1.call-start = ((), (), s32[]{:S(2)}) async-start(), calls=%async_computation.26 | async-start | bytes 589824 | tf_op jit(solution)/shard_map/reduce_scatter | solution.py:33
  154.0 6.9 collective-permute-start.12
  154.1 24.7 %collective-permute-start.13 = (bf16[128,3584]{1,0:T(8,128)(2,1)S(1)}, bf16[128,3584]{1,0:T(8,128)(2,1)}, u32[]{:S(2)}, u32[]{:S(2)}) collective-permute-start(bf16[128,3584]{1,0:T(8,128)(2,1)S(1)} %collective-permute-done.10), channel_id=1, source_target_pairs={{0,32},{32,64},{64,96},{96,128},{128,160},{160,192},{192,224},{224... | collective-permute-start | bytes 2752520 | tf_op jit(solution)/shard_map/ppermute | solution.py:10
  162.5 790.8 %reduce-scatter.39.cloned.1.call-start = ((), (), s32[]{:S(2)}) async-start(), calls=%async_computation.27 | async-start | bytes 589824 | tf_op jit(solution)/shard_map/reduce_scatter | solution.py:34
  185.0 846.7 %reduce-scatter.41.cloned.1.call-start = ((), (), s32[]{:S(2)}) async-start(), calls=%async_computation.28 | async-start | bytes 589824 | tf_op jit(solution)/shard_map/reduce_scatter | solution.py:33
  185.0 6.5 collective-permute-start.15
  185.1 23.6 %collective-permute-start.16 = (bf16[128,3584]{1,0:T(8,128)(2,1)}, bf16[128,3584]{1,0:T(8,128)(2,1)S(1)}, u32[]{:S(2)}, u32[]{:S(2)}) collective-permute-start(bf16[128,3584]{1,0:T(8,128)(2,1)} %collective-permute-done.13), channel_id=1, source_target_pairs={{0,32},{32,64},{64,96},{96,128},{128,160},{160,192},{192,224},{224... | collective-permute-start | bytes 2752520 | tf_op jit(solution)/shard_map/ppermute | solution.py:10
  193.0 917.2 %reduce-scatter.43.cloned.1.call-start = ((), (), s32[]{:S(2)}) async-start(), calls=%async_computation.29 | async-start | bytes 589824 | tf_op jit(solution)/shard_map/reduce_scatter | solution.py:34
  214.8 29.2 %copy-start.3 = (s32[128]{0:T(128)S(1)}, s32[128]{0:T(128)}, u32[]{:S(2)}) copy-start(s32[128]{0:T(128)} %param.10) | copy-start | bytes 1540
  214.8 973.6 %reduce-scatter.45.cloned.1.call-start = ((), (), s32[]{:S(2)}) async-start(), calls=%async_computation.30 | async-start | bytes 589824 | tf_op jit(solution)/shard_map/reduce_scatter | solution.py:33
  214.8 6.5 collective-permute-start.18
  214.9 22.8 %collective-permute-start.19 = (bf16[128,3584]{1,0:T(8,128)(2,1)S(1)}, bf16[128,3584]{1,0:T(8,128)(2,1)}, u32[]{:S(2)}, u32[]{:S(2)}) collective-permute-start(bf16[128,3584]{1,0:T(8,128)(2,1)S(1)} %collective-permute-done.16), channel_id=1, source_target_pairs={{0,32},{32,64},{64,96},{96,128},{128,160},{160,192},{192,224},{224... | collective-permute-start | bytes 2752520 | tf_op jit(solution)/shard_map/ppermute | solution.py:10
  222.9 1044.0 %reduce-scatter.47.cloned.1.call-start = ((), (), s32[]{:S(2)}) async-start(), calls=%async_computation.31 | async-start | bytes 589824 | tf_op jit(solution)/shard_map/reduce_scatter | solution.py:34
  244.0 3.8 collective-permute-start.2
  247.8 3.6 collective-permute-start.5
  251.4 3.6 collective-permute-start.8
  255.0 3.6 collective-permute-start.11
  258.6 3.6 collective-permute-start.14
  262.2 3.6 collective-permute-start.17
  265.8 3.6 collective-permute-start.20
Sparse Core Ops, SparseCore 0:
  11.9 77.3 reduce-scatter.16
  93.6 74.5 reduce-scatter.18
  172.0 74.3 reduce-scatter.20
  250.6 74.4 reduce-scatter.22
  328.8 74.4 reduce-scatter.24
  407.5 74.4 reduce-scatter.26
  485.8 74.4 reduce-scatter.28
  564.6 74.5 reduce-scatter.30
  643.0 74.4 reduce-scatter.32
  721.7 74.5 reduce-scatter.34
  800.1 74.4 reduce-scatter.36
  878.7 74.4 reduce-scatter.38
  957.1 74.4 reduce-scatter.40
  1035.8 74.4 reduce-scatter.42
  1113.9 74.4 reduce-scatter.44
  1192.5 74.2 reduce-scatter.46
where the time goes:
time: 1310 us
  waiting for transfers between devices  1180 us (90%)
  matrix products  61.6 us (5%)
  blocking collectives  28.7 us (2%)
  between operations  16.7 us (1%)
    reduce_scatter x8, waiting for transfers between devices, block_terms(): lax.psum_scatter(grad_gram, 'tensor', scatter_dimension=0, tiled=True)  527 us
    reduce_scatter x8, waiting for transfers between devices, block_terms(): lax.psum_scatter(act_gram, 'tensor', scatter_dimension=0, tiled=True)  464 us
    ppermute x21, waiting for transfers between devices, from_behind(): return lax.ppermute(value, axis, pairs)  191 us
    dot_general x16, matrix products, contract(): lax.dot_general(left, right, (((1,), (1,)), ((), ())), preferred_element_...  61.6 us
  transfers between devices with their start and end apart: 37, of which 34 were waited for; matrix products, arithmetic and copies ran while one was open for 5% of the time, Pallas kernels for 0%

commit v1 on v0

v1 whole, which is shorter than its diff:
```python
import functools

import jax
import jax.numpy as jnp
from jax import lax
from jax.experimental import pallas as pl
from jax.experimental.pallas import tpu as pltpu
from jax.sharding import PartitionSpec as P

LANES = 128
EXTRA = 16
STEPS = 64.0
LARGEST = 32700.0
SMALLEST = 1e-33


def contract(left, right):
    return lax.dot_general(
        left, right, (((1,), (1,)), ((), ())), preferred_element_type=jnp.float32
    )


def encode(gram):
    top = jnp.max(jnp.abs(gram), axis=0, keepdims=True)
    step = jnp.ceil(jnp.log2(jnp.maximum(top, SMALLEST) * (1.0 / LARGEST)) * STEPS)
    codes = jnp.floor(gram * jnp.exp2(step * (-1.0 / STEPS)) + 0.5)
    return codes.astype(jnp.int32).astype(jnp.int16), step.astype(jnp.int32)


def gram_kernel(n_blocks, act_ref, grad_ref, *refs):
    block_refs, out_ref, val_ref = refs[:n_blocks], refs[n_blocks], refs[n_blocks + 1]
    count = val_ref.shape[0]
    width = act_ref.shape[1]

    @pl.when(pl.program_id(0) == 0)
    def _():
        start = 0
        for ref in block_refs:
            val_ref[start : start + ref.shape[0], :] = ref[...]
            start += ref.shape[0]

    act_codes, act_step = encode(contract(val_ref[:, :width], act_ref[...]))
    grad_codes, grad_step = encode(contract(val_ref[:, width:], grad_ref[...]))
    row = lax.broadcasted_iota(jnp.int32, (EXTRA, act_step.shape[1]), 0)
    steps = jnp.where(row == 0, act_step, grad_step).astype(jnp.int16)
    for peer in range(out_ref.shape[0]):
        lanes = slice(peer * LANES, (peer + 1) * LANES)
        out_ref[peer, :count, :] = act_codes[:, lanes]
        out_ref[peer, count : 2 * count, :] = grad_codes[:, lanes]
        out_ref[peer, 2 * count :, :] = steps[:, lanes]


def grams(train_act, train_grad, blocks):
    tokens, width = train_act.shape
    hidden = train_grad.shape[1]
    count = sum(block.shape[0] for block in blocks)
    tile = 2 * LANES
    return pl.pallas_call(
        functools.partial(gram_kernel, len(blocks)),
        grid=(tokens // tile,),
        out_shape=jax.ShapeDtypeStruct(
            (tokens // LANES, 2 * count + EXTRA, LANES), jnp.int16
        ),
        in_specs=[
            pl.BlockSpec((tile, width), lambda i: (i, 0)),
            pl.BlockSpec((tile, hidden), lambda i: (i, 0)),
        ]
        + [pl.BlockSpec(block.shape, lambda i: (0, 0)) for block in blocks],
        out_specs=pl.BlockSpec(
            (tile // LANES, 2 * count + EXTRA, LANES), lambda i: (i, 0, 0)
        ),
        scratch_shapes=[pltpu.VMEM((count, width + hidden), jnp.bfloat16)],
        compiler_params=pltpu.CompilerParams(vmem_limit_bytes=32 * 2**20),
        cost_estimate=pl.CostEstimate(
            flops=2 * tokens * count * (width + hidden),
            bytes_accessed=2 * (tokens + count) * (width + hidden),
            transcendentals=0,
        ),
    )(train_act, train_grad, *blocks)


def reduce_kernel(piece_ref, out_ref):
    peers, rows, _ = piece_ref.shape
    count = (rows - EXTRA) // 2

    def total(start, which):
        result = 0.0
        for peer in range(peers):
            step = piece_ref[peer, 2 * count :, :].astype(jnp.int32).astype(jnp.float32)
            scale = jnp.exp2(step[which : which + 1, :] * (1.0 / STEPS))
            codes = piece_ref[peer, start : start + count, :]
            result += codes.astype(jnp.int32).astype(jnp.float32) * scale
        return result

    out_ref[...] = jnp.sum(total(0, 0) * total(count, 1), axis=0, keepdims=True)


def reduce(pieces):
    return pl.pallas_call(
        reduce_kernel,
        out_shape=jax.ShapeDtypeStruct((1, LANES), jnp.float32),
        compiler_params=pltpu.CompilerParams(vmem_limit_bytes=32 * 2**20),
        cost_estimate=pl.CostEstimate(
            flops=4 * pieces.size, bytes_accessed=2 * pieces.size, transcendentals=0
        ),
    )(pieces)


def per_device(train_act, train_grad, val_act, val_grad, val_mask, lengths):
    _, piece, width = train_act.shape
    train_act = train_act.reshape(piece, width)
    train_grad = train_grad.reshape(piece, train_grad.shape[2])
    ring, groups, parts = (lax.axis_size(a) for a in ("dp", "tensor", "seq"))
    val_rows = val_act.shape[0]
    scale = float(val_rows * ring) ** (-0.5)

    mask = val_mask.astype(jnp.bfloat16)[:, None]
    own = jnp.concatenate([val_act * mask, val_grad * mask], axis=1)
    core = lax.axis_index("seq") % 2
    half = val_rows // 2
    own = jnp.where(core == 0, own, jnp.concatenate([own[half:], own[:half]], axis=0))
    along = []
    for place in range(ring):
        for part in range(parts):
            other = (place + (1 if part % 2 == 0 else -1)) % ring
            along.append((place * parts + part, other * parts + part))
    swap = [(part, part ^ 1) for part in range(parts)]

    def finish(blocks):
        codes = grams(train_act, train_grad, blocks)
        return reduce(lax.all_to_all(codes, "tensor", 0, 0, tiled=True))

    moving = lax.ppermute(own, ("dp", "seq"), along)
    values = finish([own])
    for distance in range(1, ring // 2 + 1):
        here = moving
        if distance + 1 < ring // 2:
            moving = lax.ppermute(here, ("dp", "seq"), along)
        elif distance + 1 == ring // 2:
            moving = lax.ppermute(here[:half], ("dp", "seq"), along)
        values += finish([here, lax.ppermute(here, "seq", swap)])

    everyone = jnp.broadcast_to(values * scale, (groups * parts, LANES))
    everyone = lax.all_to_all(everyone, ("tensor", "seq"), 0, 0, tiled=True)
    everyone = everyone.reshape(groups, parts, LANES).transpose(1, 0, 2)
    everyone = everyone.reshape(parts, piece)
    positions = jnp.arange(parts * piece).reshape(parts, piece)
    everyone = jnp.where(positions < lengths[0], everyone, jnp.zeros_like(everyone))
    token_values = lax.dynamic_slice_in_dim(everyone, lax.axis_index("seq"), 1, axis=0)
    example_values = jnp.sum(everyone)[None] / jnp.sqrt(lengths.astype(jnp.float32))
    return (token_values, example_values)


def solution(mesh):
    return jax.shard_map(
        per_device,
        mesh=mesh,
        in_specs=(
            P("dp", "seq", "tensor"),
            P("dp", "seq", "tensor"),
            P("dp", "tensor"),
            P("dp", "tensor"),
            P("dp"),
            P("dp"),
        ),
        out_specs=(P("dp", "seq"), P("dp")),
        check_vma=False,
    )
```

time: 1310 us -> 165 us (0.13)
  waiting for transfers between devices: 1180 us -> 56.3 us
  matrix products: 61.6 us -> 0 us
  starting transfers between devices: 6.12 us -> 50.8 us
  Pallas kernels: 0 us -> 31.6 us
  blocking collectives: 28.7 us -> 0 us
  local copies, waits for them, and re-layouts: 1.54 us -> 18.2 us
  between operations: 16.7 us -> 3.25 us
    reduce_scatter x16 -> x0, waiting for transfers between devices: 991 us -> none  [the longest x8 527 us: block_terms(): lax.psum_scatter(grad_gram, 'tensor', scatter_dimension=0, tiled=True)]
    ppermute x21 -> x8, waiting for transfers between devices: 191 us -> 30 us  [the longest x2 13.5 us: per_device(): moving = lax.ppermute(here, ('dp', 'seq'), along)]
    dot_general x16 -> x0, matrix products: 61.6 us -> none  [contract(): lax.dot_general(left, right, (((1,), (1,)), ((), ())), preferred_element_...]
    all_to_all x0 -> x6, starting transfers between devices: none -> 33.4 us  [the longest x5 26.3 us: finish(): return reduce(lax.all_to_all(codes, 'tensor', 0, 0, tiled=True))]
    pallas_call x0 -> x10, Pallas kernels: none -> 31.6 us  [the longest x5 28.1 us: grams(): pl.pallas_call(functools.partial(gram_kernel, len(blocks)), grid=(tokens...]
    all_to_all x0 -> x6, waiting for transfers between devices: none -> 26.3 us  [the longest x5 19.9 us: finish(): return reduce(lax.all_to_all(codes, 'tensor', 0, 0, tiled=True))]
    all_gather x1 -> x0, blocking collectives: 16.9 us -> none  [per_device(): totals = lax.all_gather(totals, 'tensor', axis=0, tiled=True)]
    unnamed x8 -> x22, local copies, waits for them, and re-layouts: 1.54 us -> 15.7 us
  transfers between devices with their start and end apart: 37 -> 14, of which waited for: 34 -> 9; matrix products, arithmetic and copies ran while one was open for 5% -> 1% of each run, Pallas kernels for 0% -> 19%
where the time goes in v1:
time: 165 us; the launch traced here: 164 us
  waiting for transfers between devices  56.3 us (34%)
  starting transfers between devices  50.8 us (31%)
  Pallas kernels  31.6 us (19%)
  local copies, waits for them, and re-layouts  18.2 us (11%)
  other arithmetic  3.82 us (2%)
  between operations  3.25 us (2%)
    pallas_call x5, Pallas kernels, grams(): pl.pallas_call(functools.partial(gram_kernel, len(blocks)), grid=(tokens...  28.1 us
    all_to_all x5, starting transfers between devices, finish(): return reduce(lax.all_to_all(codes, 'tensor', 0, 0, tiled=True))  26.3 us
    all_to_all x5, waiting for transfers between devices, finish(): return reduce(lax.all_to_all(codes, 'tensor', 0, 0, tiled=True))  19.9 us
    unnamed x22, local copies, waits for them, and re-layouts  15.7 us
    ppermute x2, waiting for transfers between devices, per_device(): moving = lax.ppermute(here, ('dp', 'seq'), along)  13.5 us
    ppermute x1, waiting for transfers between devices, per_device(): moving = lax.ppermute(own, ('dp', 'seq'), along)  13.1 us
    all_to_all x1, starting transfers between devices, per_device(): everyone = lax.all_to_all(everyone, ('tensor', 'seq'), 0, 0, tiled=True)  7.08 us
    ppermute x1, starting transfers between devices, per_device(): moving = lax.ppermute(own, ('dp', 'seq'), along)  6.48 us
  transfers between devices with their start and end apart: 14, of which 9 were waited for; matrix products, arithmetic and copies ran while one was open for 1% of the time, Pallas kernels for 19%

profile of v1, /device:TPU:1, one launch (start us, length us, event | category | flops | bytes accessed | tf_op | source)
XLA Modules:
  0.0 164.0 jit_solution(17366275754840942973)
XLA Ops:
  0.6 0.0 copy-start.10
  0.7 0.7 convert_element_type.6
  1.4 0.0 copy-start
  1.4 1.5 broadcast_multiply_fusion
  2.8 0.0 copy-done.10
  2.8 0.1 broadcast_multiply_fusion.1
  2.9 0.1 fusion.1
  3.0 0.3 fusion.refs_0_
  3.3 6.5 %collective-permute-start = (bf16[128,4608]{1,0:T(8,128)(2,1)S(1)}, bf16[128,4608]{1,0:T(8,128)(2,1)}, u32[]{:S(2)}, u32[]{:S(2)}) collective-permute-start(bf16[128,4608]{1,0:T(8,128)(2,1)S(1)} %fusion.refs_0_), channel_id=1, source_target_pairs={{0,32},{1,225},{2,34},{3,227},{32,64},{33,1},{34,66},{35,3},{64,96... | collective-permute-start | bytes 3538952 | tf_op jit(solution)/shard_map/ppermute | solution.py:133
  9.8 13.1 %collective-permute-done.refs_0_ = bf16[128,4608]{1,0:T(8,128)(2,1)} collective-permute-done((bf16[128,4608]{1,0:T(8,128)(2,1)S(1)}, bf16[128,4608]{1,0:T(8,128)(2,1)}, u32[]{:S(2)}, u32[]{:S(2)}) %collective-permute-start) | collective-permute-done | bytes 1179680 | tf_op jit(solution)/shard_map/ppermute | solution.py:133
  22.9 3.2 %collective-permute-start.2 = (bf16[128,4608]{1,0:T(8,128)(2,1)}, bf16[128,4608]{1,0:T(8,128)(2,1)}, u32[]{:S(2)}, u32[]{:S(2)}) collective-permute-start(bf16[128,4608]{1,0:T(8,128)(2,1)} %collective-permute-done.refs_0_), channel_id=1, source_target_pairs={{0,32},{1,225},{2,34},{3,227},{32,64},{33,1},{34,66},{35,3},{64,96... | collective-permute-start | bytes 3538952 | tf_op jit(solution)/shard_map/ppermute | solution.py:138
  26.1 0.0 collective-permute-start.1
  26.1 13.5 %collective-permute-done.2.refs_0_ = bf16[128,4608]{1,0:T(8,128)(2,1)} collective-permute-done((bf16[128,4608]{1,0:T(8,128)(2,1)}, bf16[128,4608]{1,0:T(8,128)(2,1)}, u32[]{:S(2)}, u32[]{:S(2)}) %collective-permute-start.2) | collective-permute-done | bytes 1179680 | tf_op jit(solution)/shard_map/ppermute | solution.py:138
  39.6 3.1 %collective-permute-start.4 = (bf16[128,4608]{1,0:T(8,128)(2,1)}, bf16[128,4608]{1,0:T(8,128)(2,1)}, u32[]{:S(2)}, u32[]{:S(2)}) collective-permute-start(bf16[128,4608]{1,0:T(8,128)(2,1)} %collective-permute-done.2.refs_0_), channel_id=1, source_target_pairs={{0,32},{1,225},{2,34},{3,227},{32,64},{33,1},{34,66},{35,3},{64,96... | collective-permute-start | bytes 3538952 | tf_op jit(solution)/shard_map/ppermute | solution.py:138
  42.7 0.0 copy-done
  42.7 0.0 copy-start.5
  42.7 1.6 copy-done.5
  44.3 0.0 copy-start.6
  44.3 4.6 %shard_map.77 = s16[8,272,128]{2,1,0:T(8,128)(2,1)} custom-call(bf16[1024,1024]{1,0:T(8,128)(2,1)S(1)} %bitcast.18, bf16[1024,3584]{1,0:T(8,128)(2,1)S(1)} %bitcast.13, bf16[128,4608]{1,0:T(8,128)(2,1)S(1)} %fusion.refs_0_), custom_call_target="tpu_custom_call" | custom-call | flops 1207959552 | bytes 10616832 | tf_op jit(solution)/shard_map/pallas_call | solution.py:58
  48.9 6.6 %all-to-all-start = ((s16[8,272,128]{2,1,0:T(8,128)(2,1)}), s16[8,272,128]{2,1,0:T(8,128)(2,1)S(1)}, u32[]{:S(2)}, u32[]{:S(2)}) async-start(s16[8,272,128]{2,1,0:T(8,128)(2,1)} %shard_map.77), calls=%async_computation | async-start | bytes 1114112 | tf_op jit(solution)/shard_map/all_to_all | solution.py:131
  55.5 0.3 collective-permute-start.3
  55.9 0.0 collective-permute-done.1.refs_1_
  55.9 0.0 copy-done.6
  55.9 3.1 %copy-done.1 = bf16[1,1024,3584]{2,1,0:T(8,128)(2,1)S(1)} copy-done((bf16[1,1024,3584]{2,1,0:T(8,128)(2,1)S(1)}, bf16[1,1024,3584]{2,1,0:T(8,128)(2,1)}, u32[]{:S(2)}) %copy-start.1) | copy-done | bytes 7340056
  59.0 6.2 %shard_map.79 = s16[8,528,128]{2,1,0:T(8,128)(2,1)} custom-call(bf16[1024,1024]{1,0:T(8,128)(2,1)S(1)} %bitcast.19, bf16[1024,3584]{1,0:T(8,128)(2,1)S(1)} %bitcast.14, bf16[128,4608]{1,0:T(8,128)(2,1)} %collective-permute-done.refs_0_, bf16[128,4608]{1,0:T(8,128)(2,1)} %collective-permute-done.1.refs_1_), custom_call_target="tpu_custom_call" | custom-call | flops 2415919104 | bytes 11796480 | tf_op jit(solution)/shard_map/pallas_call | solution.py:58
  65.1 2.2 %all-to-all-done.piece_ref = s16[8,272,128]{2,1,0:T(8,128)(2,1)S(1)} async-done(((s16[8,272,128]{2,1,0:T(8,128)(2,1)}), s16[8,272,128]{2,1,0:T(8,128)(2,1)S(1)}, u32[]{:S(2)}, u32[]{:S(2)}) %all-to-all-start) | async-done | bytes 557088 | tf_op jit(solution)/shard_map/all_to_all | solution.py:131
  67.3 0.8 copy-done.8
  68.1 4.8 %all-to-all-start.1 = ((s16[8,528,128]{2,1,0:T(8,128)(2,1)}), s16[8,528,128]{2,1,0:T(8,128)(2,1)S(1)}, u32[]{:S(2)}, u32[]{:S(2)}) async-start(s16[8,528,128]{2,1,0:T(8,128)(2,1)} %shard_map.79), calls=%async_computation.1 | async-start | bytes 2162688 | tf_op jit(solution)/shard_map/all_to_all | solution.py:131
  72.9 0.0 collective-permute-done.4.refs_0_
  72.9 1.9 %slice.16 = bf16[64,4608]{1,0:T(8,128)(2,1)} slice(bf16[128,4608]{1,0:T(8,128)(2,1)} %collective-permute-done.4.refs_0_), slice={[0:64], [0:4608]} | slice | bytes 1179648 | tf_op jit(solution)/shard_map/slice | solution.py:140
  74.8 3.0 %collective-permute-start.6 = (bf16[64,4608]{1,0:T(8,128)(2,1)}, bf16[64,4608]{1,0:T(8,128)(2,1)}, u32[]{:S(2)}, u32[]{:S(2)}) collective-permute-start(bf16[64,4608]{1,0:T(8,128)(2,1)} %slice.16), channel_id=1, source_target_pairs={{0,32},{1,225},{2,34},{3,227},{32,64},{33,1},{34,66},{35,3},{64,96... | collective-permute-start | bytes 1769480 | tf_op jit(solution)/shard_map/ppermute | solution.py:140
  77.8 0.0 collective-permute-done.3.refs_1_
  77.8 3.1 %copy-done.2 = bf16[1,1024,3584]{2,1,0:T(8,128)(2,1)S(1)} copy-done((bf16[1,1024,3584]{2,1,0:T(8,128)(2,1)S(1)}, bf16[1,1024,3584]{2,1,0:T(8,128)(2,1)}, u32[]{:S(2)}) %copy-start.2) | copy-done | bytes 7340056
  80.9 6.2 %shard_map.81 = s16[8,528,128]{2,1,0:T(8,128)(2,1)} custom-call(bf16[1024,1024]{1,0:T(8,128)(2,1)S(1)} %bitcast.20, bf16[1024,3584]{1,0:T(8,128)(2,1)S(1)} %bitcast.15, bf16[128,4608]{1,0:T(8,128)(2,1)} %collective-permute-done.2.refs_0_, bf16[128,4608]{1,0:T(8,128)(2,1)} %collective-permute-done.3.refs_1_), custom_call_target="tpu_custom_call" | custom-call | flops 2415919104 | bytes 11796480 | tf_op jit(solution)/shard_map/pallas_call | solution.py:58
  87.1 3.2 %all-to-all-done.1.piece_ref = s16[8,528,128]{2,1,0:T(8,128)(2,1)S(1)} async-done(((s16[8,528,128]{2,1,0:T(8,128)(2,1)}), s16[8,528,128]{2,1,0:T(8,128)(2,1)S(1)}, u32[]{:S(2)}, u32[]{:S(2)}) %all-to-all-start.1) | async-done | bytes 1081376 | tf_op jit(solution)/shard_map/all_to_all | solution.py:131
  90.3 4.2 %all-to-all-start.2 = ((s16[8,528,128]{2,1,0:T(8,128)(2,1)}), s16[8,528,128]{2,1,0:T(8,128)(2,1)}, u32[]{:S(2)}, u32[]{:S(2)}) async-start(s16[8,528,128]{2,1,0:T(8,128)(2,1)} %shard_map.81), calls=%async_computation.2 | async-start | bytes 2162688 | tf_op jit(solution)/shard_map/all_to_all | solution.py:131
  94.5 1.2 collective-permute-start.5
  95.8 0.0 collective-permute-done.6.refs_0_
  95.8 0.1 collective-permute-start.7
  95.9 3.4 %collective-permute-done.7.refs_1_ = bf16[64,4608]{1,0:T(8,128)(2,1)S(1)} collective-permute-done((bf16[64,4608]{1,0:T(8,128)(2,1)}, bf16[64,4608]{1,0:T(8,128)(2,1)S(1)}, u32[]{:S(2)}, u32[]{:S(2)}) %collective-permute-start.7) | collective-permute-done | bytes 589856 | tf_op jit(solution)/shard_map/ppermute | solution.py:141
  99.3 3.1 %copy-done.3 = bf16[1,1024,3584]{2,1,0:T(8,128)(2,1)S(1)} copy-done((bf16[1,1024,3584]{2,1,0:T(8,128)(2,1)S(1)}, bf16[1,1024,3584]{2,1,0:T(8,128)(2,1)}, u32[]{:S(2)}) %copy-start.3) | copy-done | bytes 7340056
  102.4 5.0 %shard_map.85 = s16[8,272,128]{2,1,0:T(8,128)(2,1)S(1)} custom-call(bf16[1024,1024]{1,0:T(8,128)(2,1)S(1)} %bitcast.21, bf16[1024,3584]{1,0:T(8,128)(2,1)S(1)} %bitcast.16, bf16[64,4608]{1,0:T(8,128)(2,1)} %collective-permute-done.6.refs_0_, bf16[64,4608]{1,0:T(8,128)(2,1)S(1)} %collective-permute-done.7.refs_1_), custom_call_target="tpu_custom_call" | custom-call | flops 1207959552 | bytes 10616832 | tf_op jit(solution)/shard_map/pallas_call | solution.py:58
  107.4 0.0 copy-start.7
  107.4 0.8 copy-done.7
  108.2 2.4 %all-to-all-done.2.piece_ref = s16[8,528,128]{2,1,0:T(8,128)(2,1)} async-done(((s16[8,528,128]{2,1,0:T(8,128)(2,1)}), s16[8,528,128]{2,1,0:T(8,128)(2,1)}, u32[]{:S(2)}, u32[]{:S(2)}) %all-to-all-start.2) | async-done | bytes 1081376 | tf_op jit(solution)/shard_map/all_to_all | solution.py:131
  110.7 4.3 %all-to-all-start.4 = ((s16[8,272,128]{2,1,0:T(8,128)(2,1)}), s16[8,272,128]{2,1,0:T(8,128)(2,1)}, u32[]{:S(2)}, u32[]{:S(2)}) async-start(s16[8,272,128]{2,1,0:T(8,128)(2,1)} %copy-done.7), calls=%async_computation.4 | async-start | bytes 1114112 | tf_op jit(solution)/shard_map/all_to_all | solution.py:131
  115.0 0.0 collective-permute-done.5.refs_1_
  115.0 0.0 copy-start.4
  115.0 3.1 %copy-done.4 = bf16[1,1024,3584]{2,1,0:T(8,128)(2,1)S(1)} copy-done((bf16[1,1024,3584]{2,1,0:T(8,128)(2,1)S(1)}, bf16[1,1024,3584]{2,1,0:T(8,128)(2,1)}, u32[]{:S(2)}) %copy-start.4) | copy-done | bytes 7340056
  118.1 6.2 %shard_map.83 = s16[8,528,128]{2,1,0:T(8,128)(2,1)} custom-call(bf16[1024,1024]{1,0:T(8,128)(2,1)S(1)} %bitcast.22, bf16[1024,3584]{1,0:T(8,128)(2,1)S(1)} %bitcast.17, bf16[128,4608]{1,0:T(8,128)(2,1)} %collective-permute-done.4.refs_0_, bf16[128,4608]{1,0:T(8,128)(2,1)} %collective-permute-done.5.refs_1_), custom_call_target="tpu_custom_call" | custom-call | flops 2415919104 | bytes 11796480 | tf_op jit(solution)/shard_map/pallas_call | solution.py:58
  124.3 0.5 all-to-all-done.4.piece_ref
  124.8 6.3 %all-to-all-start.3 = ((s16[8,528,128]{2,1,0:T(8,128)(2,1)}), s16[8,528,128]{2,1,0:T(8,128)(2,1)S(1)}, u32[]{:S(2)}, u32[]{:S(2)}) async-start(s16[8,528,128]{2,1,0:T(8,128)(2,1)} %shard_map.83), calls=%async_computation.3 | async-start | bytes 2162688 | tf_op jit(solution)/shard_map/all_to_all | solution.py:131
  131.1 0.0 copy-done.9
  131.1 0.2 shard_map.78
  131.2 0.3 shard_map.80
  131.5 1.5 shard_map.82
  133.0 1.2 shard_map.86
  134.2 11.7 %all-to-all-done.3.piece_ref = s16[8,528,128]{2,1,0:T(8,128)(2,1)S(1)} async-done(((s16[8,528,128]{2,1,0:T(8,128)(2,1)}), s16[8,528,128]{2,1,0:T(8,128)(2,1)S(1)}, u32[]{:S(2)}, u32[]{:S(2)}) %all-to-all-start.3) | async-done | bytes 1081376 | tf_op jit(solution)/shard_map/all_to_all | solution.py:131
  145.9 0.3 shard_map.84
  146.2 0.6 broadcast_in_dim.14
  146.8 7.1 %all-to-all-start.5 = ((f32[32,1,128]{2,1,0:T(1,128)}), f32[32,1,128]{2,1,0:T(1,128)S(1)}, u32[]{:S(2)}, u32[]{:S(2)}) async-start(f32[32,1,128]{2,1,0:T(1,128)} %broadcast_in_dim.14), calls=%async_computation.5 | async-start | bytes 32768 | tf_op jit(solution)/shard_map/all_to_all | solution.py:144
  154.6 6.4 %all-to-all-done.5 = f32[32,1,128]{2,1,0:T(1,128)S(1)} async-done(((f32[32,1,128]{2,1,0:T(1,128)}), f32[32,1,128]{2,1,0:T(1,128)S(1)}, u32[]{:S(2)}, u32[]{:S(2)}) %all-to-all-start.5) | async-done | bytes 16416 | tf_op jit(solution)/shard_map/all_to_all | solution.py:144
  161.0 0.6 select_reduce_fusion
  162.2 0.6 compare_select_fusion
  (7 shorter events, 0.0 us)
Async XLA Ops:
  0.6 2.2 %copy-start.10 = (bf16[128,1024]{1,0:T(8,128)(2,1)S(1)}, bf16[128,1024]{1,0:T(8,128)(2,1)}, u32[]{:S(2)}) copy-start(bf16[128,1024]{1,0:T(8,128)(2,1)} %param.8) | copy-start | bytes 786436
  1.4 41.4 %copy-start = (bf16[1,1024,3584]{2,1,0:T(8,128)(2,1)S(1)}, bf16[1,1024,3584]{2,1,0:T(8,128)(2,1)}, u32[]{:S(2)}) copy-start(bf16[1,1024,3584]{2,1,0:T(8,128)(2,1)} %param.7) | copy-start | bytes 22020100
  3.3 19.6 %collective-permute-start = (bf16[128,4608]{1,0:T(8,128)(2,1)S(1)}, bf16[128,4608]{1,0:T(8,128)(2,1)}, u32[]{:S(2)}, u32[]{:S(2)}) collective-permute-start(bf16[128,4608]{1,0:T(8,128)(2,1)S(1)} %fusion.refs_0_), channel_id=1, source_target_pairs={{0,32},{1,225},{2,34},{3,227},{32,64},{33,1},{34,66},{35,3},{64,96... | collective-permute-start | bytes 3538952 | tf_op jit(solution)/shard_map/ppermute | solution.py:133
  22.9 16.7 %collective-permute-start.2 = (bf16[128,4608]{1,0:T(8,128)(2,1)}, bf16[128,4608]{1,0:T(8,128)(2,1)}, u32[]{:S(2)}, u32[]{:S(2)}) collective-permute-start(bf16[128,4608]{1,0:T(8,128)(2,1)} %collective-permute-done.refs_0_), channel_id=1, source_target_pairs={{0,32},{1,225},{2,34},{3,227},{32,64},{33,1},{34,66},{35,3},{64,96... | collective-permute-start | bytes 3538952 | tf_op jit(solution)/shard_map/ppermute | solution.py:138
  26.1 29.7 %collective-permute-start.1 = (bf16[128,4608]{1,0:T(8,128)(2,1)}, bf16[128,4608]{1,0:T(8,128)(2,1)}, u32[]{:S(2)}, u32[]{:S(2)}) collective-permute-start(bf16[128,4608]{1,0:T(8,128)(2,1)} %collective-permute-done.refs_0_), channel_id=1, source_target_pairs={{0,1},{1,0},{2,3},{3,2},{4,5},{5,4},{6,7},{7,6},{8,9},{9,8},{10,11... | collective-permute-start | bytes 3538952 | tf_op jit(solution)/shard_map/ppermute | solution.py:141
  39.6 33.3 %collective-permute-start.4 = (bf16[128,4608]{1,0:T(8,128)(2,1)}, bf16[128,4608]{1,0:T(8,128)(2,1)}, u32[]{:S(2)}, u32[]{:S(2)}) collective-permute-start(bf16[128,4608]{1,0:T(8,128)(2,1)} %collective-permute-done.2.refs_0_), channel_id=1, source_target_pairs={{0,32},{1,225},{2,34},{3,227},{32,64},{33,1},{34,66},{35,3},{64,96... | collective-permute-start | bytes 3538952 | tf_op jit(solution)/shard_map/ppermute | solution.py:138
  42.7 1.6 copy-start.5
  44.3 11.5 %copy-start.6 = (bf16[1,1024,1024]{2,1,0:T(8,128)(2,1)S(1)}, bf16[1,1024,1024]{2,1,0:T(8,128)(2,1)}, u32[]{:S(2)}) copy-start(bf16[1,1024,1024]{2,1,0:T(8,128)(2,1)} %param.6) | copy-start | bytes 6291460
  48.9 18.4 %all-to-all-start = ((s16[8,272,128]{2,1,0:T(8,128)(2,1)}), s16[8,272,128]{2,1,0:T(8,128)(2,1)S(1)}, u32[]{:S(2)}, u32[]{:S(2)}) async-start(s16[8,272,128]{2,1,0:T(8,128)(2,1)} %shard_map.77), calls=%async_computation | async-start | bytes 1114112 | tf_op jit(solution)/shard_map/all_to_all | solution.py:131
  55.5 22.2 %collective-permute-start.3 = (bf16[128,4608]{1,0:T(8,128)(2,1)}, bf16[128,4608]{1,0:T(8,128)(2,1)}, u32[]{:S(2)}, u32[]{:S(2)}) collective-permute-start(bf16[128,4608]{1,0:T(8,128)(2,1)} %collective-permute-done.2.refs_0_), channel_id=1, source_target_pairs={{0,1},{1,0},{2,3},{3,2},{4,5},{5,4},{6,7},{7,6},{8,9},{9,8},{10,11... | collective-permute-start | bytes 3538952 | tf_op jit(solution)/shard_map/ppermute | solution.py:141
  55.9 3.1 %copy-start.1 = (bf16[1,1024,3584]{2,1,0:T(8,128)(2,1)S(1)}, bf16[1,1024,3584]{2,1,0:T(8,128)(2,1)}, u32[]{:S(2)}) copy-start(bf16[1,1024,3584]{2,1,0:T(8,128)(2,1)} %param.7) | copy-start | bytes 22020100
  67.3 0.8 copy-start.8
  68.1 22.2 %all-to-all-start.1 = ((s16[8,528,128]{2,1,0:T(8,128)(2,1)}), s16[8,528,128]{2,1,0:T(8,128)(2,1)S(1)}, u32[]{:S(2)}, u32[]{:S(2)}) async-start(s16[8,528,128]{2,1,0:T(8,128)(2,1)} %shard_map.79), calls=%async_computation.1 | async-start | bytes 2162688 | tf_op jit(solution)/shard_map/all_to_all | solution.py:131
  74.8 21.0 %collective-permute-start.6 = (bf16[64,4608]{1,0:T(8,128)(2,1)}, bf16[64,4608]{1,0:T(8,128)(2,1)}, u32[]{:S(2)}, u32[]{:S(2)}) collective-permute-start(bf16[64,4608]{1,0:T(8,128)(2,1)} %slice.16), channel_id=1, source_target_pairs={{0,32},{1,225},{2,34},{3,227},{32,64},{33,1},{34,66},{35,3},{64,96... | collective-permute-start | bytes 1769480 | tf_op jit(solution)/shard_map/ppermute | solution.py:140
  77.8 3.1 %copy-start.2 = (bf16[1,1024,3584]{2,1,0:T(8,128)(2,1)S(1)}, bf16[1,1024,3584]{2,1,0:T(8,128)(2,1)}, u32[]{:S(2)}) copy-start(bf16[1,1024,3584]{2,1,0:T(8,128)(2,1)} %param.7) | copy-start | bytes 22020100
  90.3 20.4 %all-to-all-start.2 = ((s16[8,528,128]{2,1,0:T(8,128)(2,1)}), s16[8,528,128]{2,1,0:T(8,128)(2,1)}, u32[]{:S(2)}, u32[]{:S(2)}) async-start(s16[8,528,128]{2,1,0:T(8,128)(2,1)} %shard_map.81), calls=%async_computation.2 | async-start | bytes 2162688 | tf_op jit(solution)/shard_map/all_to_all | solution.py:131
  94.5 20.5 %collective-permute-start.5 = (bf16[128,4608]{1,0:T(8,128)(2,1)}, bf16[128,4608]{1,0:T(8,128)(2,1)}, u32[]{:S(2)}, u32[]{:S(2)}) collective-permute-start(bf16[128,4608]{1,0:T(8,128)(2,1)} %collective-permute-done.4.refs_0_), channel_id=1, source_target_pairs={{0,1},{1,0},{2,3},{3,2},{4,5},{5,4},{6,7},{7,6},{8,9},{9,8},{10,11... | collective-permute-start | bytes 3538952 | tf_op jit(solution)/shard_map/ppermute | solution.py:141
  95.8 3.5 %collective-permute-start.7 = (bf16[64,4608]{1,0:T(8,128)(2,1)}, bf16[64,4608]{1,0:T(8,128)(2,1)S(1)}, u32[]{:S(2)}, u32[]{:S(2)}) collective-permute-start(bf16[64,4608]{1,0:T(8,128)(2,1)} %collective-permute-done.6.refs_0_), channel_id=1, source_target_pairs={{0,1},{1,0},{2,3},{3,2},{4,5},{5,4},{6,7},{7,6},{8,9},{9,8},{10,11... | collective-permute-start | bytes 1769480 | tf_op jit(solution)/shard_map/ppermute | solution.py:141
  99.3 3.1 %copy-start.3 = (bf16[1,1024,3584]{2,1,0:T(8,128)(2,1)S(1)}, bf16[1,1024,3584]{2,1,0:T(8,128)(2,1)}, u32[]{:S(2)}) copy-start(bf16[1,1024,3584]{2,1,0:T(8,128)(2,1)} %param.7) | copy-start | bytes 22020100
  107.4 0.8 copy-start.7
  110.7 14.1 %all-to-all-start.4 = ((s16[8,272,128]{2,1,0:T(8,128)(2,1)}), s16[8,272,128]{2,1,0:T(8,128)(2,1)}, u32[]{:S(2)}, u32[]{:S(2)}) async-start(s16[8,272,128]{2,1,0:T(8,128)(2,1)} %copy-done.7), calls=%async_computation.4 | async-start | bytes 1114112 | tf_op jit(solution)/shard_map/all_to_all | solution.py:131
  115.0 3.1 %copy-start.4 = (bf16[1,1024,3584]{2,1,0:T(8,128)(2,1)S(1)}, bf16[1,1024,3584]{2,1,0:T(8,128)(2,1)}, u32[]{:S(2)}) copy-start(bf16[1,1024,3584]{2,1,0:T(8,128)(2,1)} %param.7) | copy-start | bytes 22020100
  124.3 6.8 %copy-start.9 = (s16[8,272,128]{2,1,0:T(8,128)(2,1)S(1)}, s16[8,272,128]{2,1,0:T(8,128)(2,1)}, u32[]{:S(2)}) copy-start(s16[8,272,128]{2,1,0:T(8,128)(2,1)} %copy-done.8) | copy-start | bytes 1671172
  124.8 21.2 %all-to-all-start.3 = ((s16[8,528,128]{2,1,0:T(8,128)(2,1)}), s16[8,528,128]{2,1,0:T(8,128)(2,1)S(1)}, u32[]{:S(2)}, u32[]{:S(2)}) async-start(s16[8,528,128]{2,1,0:T(8,128)(2,1)} %shard_map.83), calls=%async_computation.3 | async-start | bytes 2162688 | tf_op jit(solution)/shard_map/all_to_all | solution.py:131
  146.8 14.1 %all-to-all-start.5 = ((f32[32,1,128]{2,1,0:T(1,128)}), f32[32,1,128]{2,1,0:T(1,128)S(1)}, u32[]{:S(2)}, u32[]{:S(2)}) async-start(f32[32,1,128]{2,1,0:T(1,128)} %broadcast_in_dim.14), calls=%async_computation.5 | async-start | bytes 32768 | tf_op jit(solution)/shard_map/all_to_all | solution.py:144

commit v2 on v0

v2 whole, which is shorter than its diff:
```python
import functools

import jax
import jax.numpy as jnp
from jax import lax
from jax.experimental import pallas as pl
from jax.experimental.pallas import tpu as pltpu
from jax.sharding import PartitionSpec as P

LANES = 128
TILE = 256
EXTRA = 16
STEPS = 64.0
LARGEST = 32700.0
SMALLEST = 1e-33
IN_VMEM = pl.BlockSpec(memory_space=pltpu.VMEM)
IN_SMEM = pl.BlockSpec(memory_space=pltpu.SMEM)


def kernel_call(
    kernel, name, out_shape, in_specs, out_specs, moved, scratch=(), grant=4
):
    return pl.pallas_call(
        kernel,
        name=name,
        out_shape=out_shape,
        in_specs=in_specs,
        out_specs=out_specs,
        scratch_shapes=scratch,
        compiler_params=pltpu.CompilerParams(vmem_limit_bytes=grant * 2**20),
        cost_estimate=pl.CostEstimate(flops=0, bytes_accessed=moved, transcendentals=0),
    )


def contract(left, right):
    return lax.dot_general(
        left, right, (((1,), (1,)), ((), ())), preferred_element_type=jnp.float32
    )


def prepare_kernel(core_ref, mask_in, act_in, grad_in, *refs):
    out_ref, mask_ref, act_ref, grad_ref, sems = refs
    copies = [
        pltpu.make_async_copy(source, target, sems.at[index])
        for index, (source, target) in enumerate(
            ((mask_in, mask_ref), (act_in, act_ref), (grad_in, grad_ref))
        )
    ]
    for copy in copies:
        copy.start()
    for copy in copies:
        copy.wait()
    rows, width = act_ref.shape
    half = rows // 2
    row = lax.broadcasted_iota(jnp.int32, (rows, rows), 0)
    column = lax.broadcasted_iota(jnp.int32, (rows, rows), 1)
    mask = jnp.where(row == column, mask_ref[...].astype(jnp.float32), 0.0)
    mask = jnp.sum(mask, axis=1, keepdims=True)
    for part in range(2):
        place = pl.multiple_of(jnp.where(core_ref[0] == part, 0, half), half)
        rows_in = slice(part * half, (part + 1) * half)
        factor = mask[rows_in].astype(jnp.bfloat16)
        out_ref[pl.ds(place, half), :width] = act_ref[rows_in, :] * factor
        out_ref[pl.ds(place, half), width:] = grad_ref[rows_in, :] * factor


def prepare(core, mask, act, grad):
    rows, width = act.shape
    shape = (rows, width + grad.shape[1])
    arrays = [pltpu.with_memory_space_constraint(a, pltpu.HBM) for a in (mask, act, grad)]
    return kernel_call(
        prepare_kernel,
        "prepare",
        jax.ShapeDtypeStruct(shape, act.dtype),
        [IN_SMEM] + [pl.BlockSpec(memory_space=pltpu.HBM)] * 3,
        IN_VMEM,
        8 * rows * shape[1],
        [pltpu.VMEM(a.shape, a.dtype) for a in arrays]
        + [pltpu.SemaphoreType.DMA((3,))],
        8,
    )(core, *arrays)


def encode(gram):
    top = jnp.max(jnp.abs(gram), axis=0, keepdims=True)
    step = jnp.ceil(jnp.log2(jnp.maximum(top, SMALLEST) * (1.0 / LARGEST)) * STEPS)
    codes = jnp.floor(gram * jnp.exp2(step * (-1.0 / STEPS)) + 0.5)
    return codes.astype(jnp.int32).astype(jnp.int16), step.astype(jnp.int32)


def gram_kernel(n_blocks, n_before, act_ref, grad_ref, *refs):
    block_refs, refs = refs[:n_blocks], refs[n_blocks:]
    before_refs, (out_ref, val_ref, code_ref, sems) = refs[:n_before], refs[n_before:]
    start = 0
    for ref in block_refs:
        val_ref[start : start + ref.shape[0], :] = ref[...]
        start += ref.shape[0]
    count = val_ref.shape[0]
    tokens, width = act_ref.shape
    each = TILE // LANES
    for ref in before_refs:
        code_ref[:, 2 * count + EXTRA :, :] = ref[...]
    copies = []
    for tile in range(tokens // TILE):
        rows = slice(tile * TILE, (tile + 1) * TILE)
        act_codes, act_step = encode(contract(val_ref[:, :width], act_ref[rows, :]))
        grad_codes, grad_step = encode(contract(val_ref[:, width:], grad_ref[rows, :]))
        row = lax.broadcasted_iota(jnp.int32, (EXTRA, TILE), 0)
        steps = jnp.where(row == 0, act_step, grad_step).astype(jnp.int16)
        for part in range(each):
            peer = tile * each + part
            lanes = slice(part * LANES, (part + 1) * LANES)
            code_ref[peer, :count, :] = act_codes[:, lanes]
            code_ref[peer, count : 2 * count, :] = grad_codes[:, lanes]
            code_ref[peer, 2 * count : 2 * count + EXTRA, :] = steps[:, lanes]
        peers = pl.ds(tile * each, each)
        copies.append(
            pltpu.make_async_copy(code_ref.at[peers], out_ref.at[peers], sems.at[tile])
        )
        copies[-1].start()
    for copy in copies:
        copy.wait()


def grams(train, blocks, before=(), place=pltpu.HBM):
    tokens = train[0].shape[0]
    width = train[0].shape[1] + train[1].shape[1]
    count = sum(block.shape[0] for block in blocks)
    rows = 2 * count + EXTRA + sum(codes.shape[1] for codes in before)
    shape = (tokens // LANES, rows, LANES)
    return kernel_call(
        functools.partial(gram_kernel, len(blocks), len(before)),
        "grams",
        place(shape, jnp.int16),
        [IN_VMEM] * (2 + len(blocks) + len(before)),
        pl.BlockSpec(memory_space=place),
        4 * tokens * count,
        [
            pltpu.VMEM((count, width), jnp.bfloat16),
            pltpu.VMEM(shape, jnp.int16),
            pltpu.SemaphoreType.DMA((tokens // TILE,)),
        ],
        12,
    )(*train, *blocks, *before)


def reduce_kernel(counts, scale, before_ref, piece_ref, out_ref):
    sums, start = before_ref[...], 0

    def total(first, count, which, steps):
        result = 0.0
        for peer in range(piece_ref.shape[0]):
            step = piece_ref[peer, steps : steps + EXTRA, :].astype(jnp.int32)
            step = step[which : which + 1, :].astype(jnp.float32)
            codes = piece_ref[peer, first : first + count, :]
            codes = codes.astype(jnp.int32).astype(jnp.float32)
            result += codes * jnp.exp2(step * (1.0 / STEPS))
        return result

    for count in counts:
        steps = start + 2 * count
        act = total(start, count, 0, steps)
        grad = total(start + count, count, 1, steps)
        sums += jnp.sum(act * grad, axis=0, keepdims=True)
        start = steps + EXTRA
    out_ref[...] = jnp.broadcast_to(sums * scale, out_ref.shape)


def reduce(before, pieces, counts, scale=1.0, copies=1):
    return kernel_call(
        functools.partial(reduce_kernel, counts, scale),
        "reduce",
        jax.ShapeDtypeStruct((copies, LANES), jnp.float32),
        [IN_VMEM, IN_VMEM],
        IN_VMEM,
        2 * pieces.size,
    )(before, pieces)


def finish_kernel(parts, seq_ref, length_ref, all_ref, token_ref, example_ref):
    rows = all_ref.shape[0]
    groups = rows // parts
    row = lax.broadcasted_iota(jnp.int32, (rows, LANES), 0)
    lane = lax.broadcasted_iota(jnp.int32, (rows, LANES), 1)
    position = ((row % parts) * groups + row // parts) * LANES + lane
    values = jnp.where(position < length_ref[0], all_ref[...], 0.0)
    for group in range(groups):
        group_values = values[group * parts : (group + 1) * parts]
        part = lax.broadcasted_iota(jnp.int32, (parts, LANES), 0)
        own = jnp.where(part == seq_ref[0], group_values, 0.0)
        token_ref[:, group * LANES : (group + 1) * LANES] = jnp.sum(
            own, axis=0, keepdims=True
        )
    total = jnp.sum(jnp.sum(values, axis=0, keepdims=True), axis=1, keepdims=True)
    length = jnp.full((1, 1), length_ref[0], jnp.int32).astype(jnp.float32)
    example_ref[0] = (total / jnp.sqrt(length))[0, 0]


def finish(parts, seq, lengths, everyone):
    return kernel_call(
        functools.partial(finish_kernel, parts),
        "finish",
        (
            jax.ShapeDtypeStruct((1, everyone.size // parts), jnp.float32),
            jax.ShapeDtypeStruct((1,), jnp.float32),
        ),
        [IN_SMEM, IN_SMEM, IN_VMEM],
        (IN_VMEM, IN_SMEM),
        4 * everyone.size,
    )(seq, lengths, everyone)


def per_device(train_act, train_grad, val_act, val_grad, val_mask, lengths):
    _, piece, width = train_act.shape
    train_act = train_act.reshape(piece, width)
    train_grad = train_grad.reshape(piece, train_grad.shape[2])
    ring, groups, parts = (lax.axis_size(a) for a in ("dp", "tensor", "seq"))
    val_rows = val_act.shape[0]
    scale = float(val_rows * ring) ** (-0.5)
    seq = lax.axis_index("seq").astype(jnp.int32).reshape(1)

    own = prepare(seq & 1, val_mask.reshape(1, val_rows), val_act, val_grad)
    own, half = [own], val_rows // 2
    along = []
    for place in range(ring):
        for part in range(parts):
            other = (place + (1 if part % 2 == 0 else -1)) % ring
            along.append((place * parts + part, other * parts + part))
    swap = [(part, part ^ 1) for part in range(parts)]

    def pass_on(blocks):
        return [lax.ppermute(block, ("dp", "seq"), along) for block in blocks]

    train = (train_act, train_grad)
    last = ring // 2
    moving = pass_on(own)
    codes = grams(train, own, (), pltpu.VMEM)
    own_codes, waiting, sent = codes, [], []
    for distance in range(1, last + 1):
        here, codes, own_codes = lax.optimization_barrier((moving, codes, own_codes))
        if distance < last - 2:
            moving = pass_on(here)
        elif distance == last - 2:
            moving = pass_on([here[0][:half], here[0][half:]])
        elif distance == last - 1:
            moving = pass_on(here[:1])
        waiting += here + [lax.ppermute(block, "seq", swap) for block in here]
        if distance == last - 1:
            continue
        counts, before = (sum(block.shape[0] for block in waiting),), ()
        if distance == 1:
            counts, before = counts + (val_rows,), (own_codes,)
        codes, waiting = grams(train, waiting, before), []
        sent.append((counts, lax.all_to_all(codes, "tensor", 0, 0, tiled=True)))
    values = jnp.zeros((1, LANES), jnp.float32)
    values, codes = lax.optimization_barrier((values, codes))
    for counts, pieces in sent[:-1]:
        values = reduce(values, pieces, counts)
    counts, pieces = sent[-1]
    everyone = reduce(values, pieces, counts, scale, groups * parts)

    everyone = lax.all_to_all(everyone, ("tensor", "seq"), 0, 0, tiled=True)
    return finish(parts, seq, lengths, everyone)


def solution(mesh):
    return jax.shard_map(
        per_device,
        mesh=mesh,
        in_specs=(
            P("dp", "seq", "tensor"),
            P("dp", "seq", "tensor"),
            P("dp", "tensor"),
            P("dp", "tensor"),
            P("dp"),
            P("dp"),
        ),
        out_specs=(P("dp", "seq"), P("dp")),
        check_vma=False,
    )
```

time: 1310 us -> 126 us (0.10)
  waiting for transfers between devices: 1180 us -> 43.8 us
  matrix products: 61.6 us -> 0 us
  starting transfers between devices: 6.12 us -> 42.9 us
  blocking collectives: 28.7 us -> 0 us
  Pallas kernels: 0 us -> 28.2 us
  between operations: 16.7 us -> 1.54 us
    reduce_scatter x16 -> x0, waiting for transfers between devices: 991 us -> none  [the longest x8 527 us: block_terms(): lax.psum_scatter(grad_gram, 'tensor', scatter_dimension=0, tiled=True)]
    ppermute x21 -> x10, waiting for transfers between devices: 191 us -> 14.4 us  [the longest x5 10.5 us: pass_on(): return [lax.ppermute(block, ('dp', 'seq'), along) for block in blocks]]
    dot_general x16 -> x0, matrix products: 61.6 us -> none  [contract(): lax.dot_general(left, right, (((1,), (1,)), ((), ())), preferred_element_...]
    all_to_all x0 -> x4, waiting for transfers between devices: none -> 29.5 us  [the longest x3 23.1 us: per_device(): sent.append((counts, lax.all_to_all(codes, 'tensor', 0, 0, tiled=True)))]
    pallas_call x0 -> x9, Pallas kernels: none -> 28.2 us  [the longest x4 22.7 us: grams(): kernel_call(functools.partial(gram_kernel, len(blocks), len(before)), 'gr...]
    all_to_all x0 -> x4, starting transfers between devices: none -> 22.2 us  [the longest x3 17.2 us: per_device(): sent.append((counts, lax.all_to_all(codes, 'tensor', 0, 0, tiled=True)))]
    all_gather x1 -> x0, blocking collectives: 16.9 us -> none  [per_device(): totals = lax.all_gather(totals, 'tensor', axis=0, tiled=True)]
    ppermute x21 -> x10, starting transfers between devices: 5.46 us -> 20.7 us  [the longest x5 11.4 us: pass_on(): return [lax.ppermute(block, ('dp', 'seq'), along) for block in blocks]]
  transfers between devices with their start and end apart: 37 -> 14, of which waited for: 34 -> 9; matrix products, arithmetic and copies ran while one was open for 5% -> 0% of each run, Pallas kernels for 0% -> 20%
where the time goes in v2:
time: 126 us
  waiting for transfers between devices  43.8 us (35%)
  starting transfers between devices  42.9 us (34%)
  Pallas kernels  28.2 us (22%)
  local copies, waits for them, and re-layouts  9.41 us (7%)
  between operations  1.54 us (1%)
    all_to_all x3, waiting for transfers between devices, per_device(): sent.append((counts, lax.all_to_all(codes, 'tensor', 0, 0, tiled=True)))  23.1 us
    pallas_call x4, Pallas kernels, grams(): kernel_call(functools.partial(gram_kernel, len(blocks), len(before)), 'gr...  22.7 us
    all_to_all x3, starting transfers between devices, per_device(): sent.append((counts, lax.all_to_all(codes, 'tensor', 0, 0, tiled=True)))  17.2 us
    ppermute x5, starting transfers between devices, pass_on(): return [lax.ppermute(block, ('dp', 'seq'), along) for block in blocks]  11.4 us
    ppermute x5, waiting for transfers between devices, pass_on(): return [lax.ppermute(block, ('dp', 'seq'), along) for block in blocks]  10.5 us
    ppermute x5, starting transfers between devices, per_device(): waiting += here + [lax.ppermute(block, 'seq', swap) for block in here]  9.34 us
    unnamed x10, local copies, waits for them, and re-layouts  9.33 us
    all_to_all x1, waiting for transfers between devices, per_device(): everyone = lax.all_to_all(everyone, ('tensor', 'seq'), 0, 0, tiled=True)  6.4 us
  transfers between devices with their start and end apart: 14, of which 9 were waited for; matrix products, arithmetic and copies ran while one was open for 0% of the time, Pallas kernels for 20%

profile of v2, /device:TPU:1, one launch (start us, length us, event | category | flops | bytes accessed | tf_op | source)
XLA Modules:
  0.0 125.9 jit_solution(16273164310244452151)
XLA Ops:
  0.6 0.0 copy-start.4
  0.6 1.6 %prepare.1.refs_0_ = bf16[128,4608]{1,0:T(8,128)(2,1)S(1)} custom-call(s32[1]{0:T(128)S(6)} %and.4.core_ref, s32[1,128]{1,0:T(1,128)} %bitcast.17, bf16[128,1024]{1,0:T(8,128)(2,1)} %act_in.1, bf16[128,3584]{1,0:T(8,128)(2,1)} %grad_in.1), custom_call_target="tpu_custom_call" | custom-call | bytes 4718592 | tf_op jit(solution)/shard_map/prepare/pallas_call | solution.py:71
  2.3 6.5 %collective-permute-start = (bf16[128,4608]{1,0:T(8,128)(2,1)S(1)}, bf16[128,4608]{1,0:T(8,128)(2,1)}, u32[]{:S(2)}, u32[]{:S(2)}) collective-permute-start(bf16[128,4608]{1,0:T(8,128)(2,1)S(1)} %prepare.1.refs_0_), channel_id=1, source_target_pairs={{0,32},{1,225},{2,34},{3,227},{32,64},{33,1},{34,66},{35,3},{64,96... | collective-permute-start | bytes 3538952 | tf_op jit(solution)/shard_map/ppermute | solution.py:232
  8.7 0.0 copy-done.4
  8.7 0.0 copy-start
  8.7 3.1 %copy-done = bf16[1,1024,3584]{2,1,0:T(8,128)(2,1)S(1)} copy-done((bf16[1,1024,3584]{2,1,0:T(8,128)(2,1)S(1)}, bf16[1,1024,3584]{2,1,0:T(8,128)(2,1)}, u32[]{:S(2)}) %copy-start) | copy-done | bytes 7340056
  11.9 0.0 copy-start.1
  11.9 6.6 %grams.4.refs_2_ = s16[8,272,128]{2,1,0:T(8,128)(2,1)S(1)} custom-call(bf16[1024,1024]{1,0:T(8,128)(2,1)S(1)} %bitcast.12, bf16[1024,3584]{1,0:T(8,128)(2,1)S(1)} %bitcast.8, bf16[128,4608]{1,0:T(8,128)(2,1)S(1)} %prepare.1.refs_0_), custom_call_target="tpu_custom_call" | custom-call | bytes 524288 | tf_op jit(solution)/shard_map/grams/pallas_call | solution.py:131
  18.4 3.5 %collective-permute-done.refs_0_ = bf16[128,4608]{1,0:T(8,128)(2,1)} collective-permute-done((bf16[128,4608]{1,0:T(8,128)(2,1)S(1)}, bf16[128,4608]{1,0:T(8,128)(2,1)}, u32[]{:S(2)}, u32[]{:S(2)}) %collective-permute-start) | collective-permute-done | bytes 1179680 | tf_op jit(solution)/shard_map/ppermute | solution.py:232
  21.9 2.1 %collective-permute-start.2 = (bf16[128,4608]{1,0:T(8,128)(2,1)}, bf16[128,4608]{1,0:T(8,128)(2,1)S(1)}, u32[]{:S(2)}, u32[]{:S(2)}) collective-permute-start(bf16[128,4608]{1,0:T(8,128)(2,1)} %collective-permute-done.refs_0_), channel_id=1, source_target_pairs={{0,1},{1,0},{2,3},{3,2},{4,5},{5,4},{6,7},{7,6},{8,9},{9,8},{10,11... | collective-permute-start | bytes 3538952 | tf_op jit(solution)/shard_map/ppermute | solution.py:247
  24.0 1.7 %collective-permute-start.1 = (bf16[128,4608]{1,0:T(8,128)(2,1)}, bf16[128,4608]{1,0:T(8,128)(2,1)S(1)}, u32[]{:S(2)}, u32[]{:S(2)}) collective-permute-start(bf16[128,4608]{1,0:T(8,128)(2,1)} %collective-permute-done.refs_0_), channel_id=1, source_target_pairs={{0,32},{1,225},{2,34},{3,227},{32,64},{33,1},{34,66},{35,3},{64,96... | collective-permute-start | bytes 3538952 | tf_op jit(solution)/shard_map/ppermute | solution.py:232
  25.7 0.9 collective-permute-done.2.refs_1_
  26.7 0.0 copy-done.1
  26.7 5.3 %grams.5 = s16[8,800,128]{2,1,0:T(8,128)(2,1)} custom-call(bf16[1024,1024]{1,0:T(8,128)(2,1)S(1)} %bitcast.13, bf16[1024,3584]{1,0:T(8,128)(2,1)S(1)} %bitcast.9, bf16[128,4608]{1,0:T(8,128)(2,1)} %collective-permute-done.refs_0_, bf16[128,4608]{1,0:T(8,128)(2,1)S(1)} %collective-permute-done.2.refs_1_, s16[8,272,128]{2,1,0:T(8,128)(2,1)S(1)} %grams.4.refs_2_), custom_call_target="tpu_custom_call" | custom-call | bytes 1048576 | tf_op jit(solution)/shard_map/grams/pallas_call | solution.py:131
  31.9 6.7 %all-to-all-start = ((s16[8,800,128]{2,1,0:T(8,128)(2,1)}), s16[8,800,128]{2,1,0:T(8,128)(2,1)}, u32[]{:S(2)}, u32[]{:S(2)}) async-start(s16[8,800,128]{2,1,0:T(8,128)(2,1)} %grams.5), calls=%async_computation | async-start | bytes 3276800 | tf_op jit(solution)/shard_map/all_to_all | solution.py:254
  38.6 0.9 collective-permute-done.1.refs_0_
  39.5 2.1 %collective-permute-start.5 = (bf16[128,4608]{1,0:T(8,128)(2,1)S(1)}, bf16[128,4608]{1,0:T(8,128)(2,1)S(1)}, u32[]{:S(2)}, u32[]{:S(2)}) collective-permute-start(bf16[128,4608]{1,0:T(8,128)(2,1)S(1)} %collective-permute-done.1.refs_0_), channel_id=1, source_target_pairs={{0,1},{1,0},{2,3},{3,2},{4,5},{5,4},{6,7},{7,6},{8,9},{9,8},{10,11... | collective-permute-start | bytes 3538952 | tf_op jit(solution)/shard_map/ppermute | solution.py:247
  41.6 0.1 fusion
  41.7 0.7 collective-permute-start.3
  42.4 0.7 collective-permute-start.4
  43.0 1.1 collective-permute-done.5.refs_1_
  44.1 0.0 copy-start.2
  44.1 3.1 %copy-done.2 = bf16[1,1024,3584]{2,1,0:T(8,128)(2,1)S(1)} copy-done((bf16[1,1024,3584]{2,1,0:T(8,128)(2,1)S(1)}, bf16[1,1024,3584]{2,1,0:T(8,128)(2,1)}, u32[]{:S(2)}) %copy-start.2) | copy-done | bytes 7340056
  47.2 3.9 %grams.6 = s16[8,528,128]{2,1,0:T(8,128)(2,1)} custom-call(bf16[1024,1024]{1,0:T(8,128)(2,1)S(1)} %bitcast.14, bf16[1024,3584]{1,0:T(8,128)(2,1)S(1)} %bitcast.10, bf16[128,4608]{1,0:T(8,128)(2,1)S(1)} %collective-permute-done.1.refs_0_, bf16[128,4608]{1,0:T(8,128)(2,1)S(1)} %collective-permute-done.5.refs_1_), custom_call_target="tpu_custom_call" | custom-call | bytes 1048576 | tf_op jit(solution)/shard_map/grams/pallas_call | solution.py:131
  51.1 0.0 collective-permute-done.3.refs_0_
  51.1 6.1 %collective-permute-done.4.refs_1_ = bf16[64,4608]{1,0:T(8,128)(2,1)} collective-permute-done((bf16[64,4608]{1,0:T(8,128)(2,1)S(1)}, bf16[64,4608]{1,0:T(8,128)(2,1)}, u32[]{:S(2)}, u32[]{:S(2)}) %collective-permute-start.4) | collective-permute-done | bytes 589856 | tf_op jit(solution)/shard_map/ppermute | solution.py:232
  57.2 1.8 %collective-permute-start.8 = (bf16[64,4608]{1,0:T(8,128)(2,1)}, bf16[64,4608]{1,0:T(8,128)(2,1)}, u32[]{:S(2)}, u32[]{:S(2)}) collective-permute-start(bf16[64,4608]{1,0:T(8,128)(2,1)} %collective-permute-done.3.refs_0_), channel_id=1, source_target_pairs={{0,32},{1,225},{2,34},{3,227},{32,64},{33,1},{34,66},{35,3},{64,96... | collective-permute-start | bytes 1769480 | tf_op jit(solution)/shard_map/ppermute | solution.py:232
  59.0 2.6 %all-to-all-done.piece_ref = s16[8,800,128]{2,1,0:T(8,128)(2,1)} async-done(((s16[8,800,128]{2,1,0:T(8,128)(2,1)}), s16[8,800,128]{2,1,0:T(8,128)(2,1)}, u32[]{:S(2)}, u32[]{:S(2)}) %all-to-all-start) | async-done | bytes 1638432 | tf_op jit(solution)/shard_map/all_to_all | solution.py:254
  61.7 3.9 %all-to-all-start.1 = ((s16[8,528,128]{2,1,0:T(8,128)(2,1)}), s16[8,528,128]{2,1,0:T(8,128)(2,1)S(1)}, u32[]{:S(2)}, u32[]{:S(2)}) async-start(s16[8,528,128]{2,1,0:T(8,128)(2,1)} %grams.6), calls=%async_computation.1 | async-start | bytes 2162688 | tf_op jit(solution)/shard_map/all_to_all | solution.py:254
  65.5 1.4 %collective-permute-start.6 = (bf16[64,4608]{1,0:T(8,128)(2,1)}, bf16[64,4608]{1,0:T(8,128)(2,1)S(1)}, u32[]{:S(2)}, u32[]{:S(2)}) collective-permute-start(bf16[64,4608]{1,0:T(8,128)(2,1)} %collective-permute-done.3.refs_0_), channel_id=1, source_target_pairs={{0,1},{1,0},{2,3},{3,2},{4,5},{5,4},{6,7},{7,6},{8,9},{9,8},{10,11... | collective-permute-start | bytes 1769480 | tf_op jit(solution)/shard_map/ppermute | solution.py:247
  66.9 0.1 collective-permute-start.7
  67.0 0.0 collective-permute-done.8.refs_4_
  67.0 3.7 %collective-permute-start.9 = (bf16[64,4608]{1,0:T(8,128)(2,1)}, bf16[64,4608]{1,0:T(8,128)(2,1)S(1)}, u32[]{:S(2)}, u32[]{:S(2)}) collective-permute-start(bf16[64,4608]{1,0:T(8,128)(2,1)} %collective-permute-done.8.refs_4_), channel_id=1, source_target_pairs={{0,1},{1,0},{2,3},{3,2},{4,5},{5,4},{6,7},{7,6},{8,9},{9,8},{10,11... | collective-permute-start | bytes 1769480 | tf_op jit(solution)/shard_map/ppermute | solution.py:247
  70.7 0.0 collective-permute-done.6.refs_2_
  70.7 0.0 collective-permute-done.7.refs_3_
  70.7 1.8 %collective-permute-done.9.refs_5_ = bf16[64,4608]{1,0:T(8,128)(2,1)S(1)} collective-permute-done((bf16[64,4608]{1,0:T(8,128)(2,1)}, bf16[64,4608]{1,0:T(8,128)(2,1)S(1)}, u32[]{:S(2)}, u32[]{:S(2)}) %collective-permute-start.9) | collective-permute-done | bytes 589856 | tf_op jit(solution)/shard_map/ppermute | solution.py:247
  72.6 0.0 copy-start.3
  72.6 3.1 %copy-done.3 = bf16[1,1024,3584]{2,1,0:T(8,128)(2,1)S(1)} copy-done((bf16[1,1024,3584]{2,1,0:T(8,128)(2,1)S(1)}, bf16[1,1024,3584]{2,1,0:T(8,128)(2,1)}, u32[]{:S(2)}) %copy-start.3) | copy-done | bytes 7340056
  75.7 7.0 %grams.7 = s16[8,784,128]{2,1,0:T(8,128)(2,1)} custom-call(bf16[1024,1024]{1,0:T(8,128)(2,1)S(1)} %bitcast.15, bf16[1024,3584]{1,0:T(8,128)(2,1)S(1)} %bitcast.11, bf16[64,4608]{1,0:T(8,128)(2,1)} %collective-permute-done.3.refs_0_, bf16[64,4608]{1,0:T(8,128)(2,1)} %collective-permute-done.4.refs_1_, bf16[64,4608]{1,0:T(8,128)(2,1)S(1)} %collective-permute-done.6.refs_2_, ...), custom_call_target="tpu_custom_call" | custom-call | bytes 1572864 | tf_op jit(solution)/shard_map/grams/pallas_call | solution.py:131
  82.6 0.0 all-to-all-done.1.piece_ref
  82.6 6.7 %all-to-all-start.2 = ((s16[8,784,128]{2,1,0:T(8,128)(2,1)}), s16[8,784,128]{2,1,0:T(8,128)(2,1)S(1)}, u32[]{:S(2)}, u32[]{:S(2)}) async-start(s16[8,784,128]{2,1,0:T(8,128)(2,1)} %grams.7), calls=%async_computation.2 | async-start | bytes 3211264 | tf_op jit(solution)/shard_map/all_to_all | solution.py:254
  89.3 1.9 %reduce.3.before_ref = f32[1,128]{1,0:T(1,128)S(1)} custom-call(f32[1,128]{1,0:T(1,128)S(1)} %broadcast_in_dim.3.before_ref, s16[8,800,128]{2,1,0:T(8,128)(2,1)} %all-to-all-done.piece_ref), custom_call_target="tpu_custom_call" | custom-call | bytes 1638400 | tf_op jit(solution)/shard_map/reduce/pallas_call | solution.py:170
  91.2 0.3 reduce.4.before_ref
  91.5 20.4 %all-to-all-done.2.piece_ref = s16[8,784,128]{2,1,0:T(8,128)(2,1)S(1)} async-done(((s16[8,784,128]{2,1,0:T(8,128)(2,1)}), s16[8,784,128]{2,1,0:T(8,128)(2,1)S(1)}, u32[]{:S(2)}, u32[]{:S(2)}) %all-to-all-start.2) | async-done | bytes 1605664 | tf_op jit(solution)/shard_map/all_to_all | solution.py:254
  111.9 1.1 reduce.5
  113.0 5.0 %all-to-all-start.3 = ((f32[32,1,128]{2,1,0:T(1,128)}), f32[32,1,128]{2,1,0:T(1,128)S(1)}, u32[]{:S(2)}, u32[]{:S(2)}) async-start(f32[32,1,128]{2,1,0:T(1,128)} %bitcast.5), calls=%async_computation.3 | async-start | bytes 32768 | tf_op jit(solution)/shard_map/all_to_all | solution.py:262
  118.7 6.4 %all-to-all-done.3 = f32[32,1,128]{2,1,0:T(1,128)S(1)} async-done(((f32[32,1,128]{2,1,0:T(1,128)}), f32[32,1,128]{2,1,0:T(1,128)S(1)}, u32[]{:S(2)}, u32[]{:S(2)}) %all-to-all-start.3) | async-done | bytes 16416 | tf_op jit(solution)/shard_map/all_to_all | solution.py:262
  125.1 0.6 finish.1
  (1 shorter events, 0.0 us)
Async XLA Ops:
  0.6 8.1 %copy-start.4 = (bf16[1,1024,1024]{2,1,0:T(8,128)(2,1)S(1)}, bf16[1,1024,1024]{2,1,0:T(8,128)(2,1)}, u32[]{:S(2)}) copy-start(bf16[1,1024,1024]{2,1,0:T(8,128)(2,1)} %param.6) | copy-start | bytes 6291460
  2.3 19.6 %collective-permute-start = (bf16[128,4608]{1,0:T(8,128)(2,1)S(1)}, bf16[128,4608]{1,0:T(8,128)(2,1)}, u32[]{:S(2)}, u32[]{:S(2)}) collective-permute-start(bf16[128,4608]{1,0:T(8,128)(2,1)S(1)} %prepare.1.refs_0_), channel_id=1, source_target_pairs={{0,32},{1,225},{2,34},{3,227},{32,64},{33,1},{34,66},{35,3},{64,96... | collective-permute-start | bytes 3538952 | tf_op jit(solution)/shard_map/ppermute | solution.py:232
  8.7 3.1 %copy-start = (bf16[1,1024,3584]{2,1,0:T(8,128)(2,1)S(1)}, bf16[1,1024,3584]{2,1,0:T(8,128)(2,1)}, u32[]{:S(2)}) copy-start(bf16[1,1024,3584]{2,1,0:T(8,128)(2,1)} %param.7) | copy-start | bytes 22020100
  11.9 14.8 %copy-start.1 = (bf16[1,1024,3584]{2,1,0:T(8,128)(2,1)S(1)}, bf16[1,1024,3584]{2,1,0:T(8,128)(2,1)}, u32[]{:S(2)}) copy-start(bf16[1,1024,3584]{2,1,0:T(8,128)(2,1)} %param.7) | copy-start | bytes 22020100
  21.9 4.8 %collective-permute-start.2 = (bf16[128,4608]{1,0:T(8,128)(2,1)}, bf16[128,4608]{1,0:T(8,128)(2,1)S(1)}, u32[]{:S(2)}, u32[]{:S(2)}) collective-permute-start(bf16[128,4608]{1,0:T(8,128)(2,1)} %collective-permute-done.refs_0_), channel_id=1, source_target_pairs={{0,1},{1,0},{2,3},{3,2},{4,5},{5,4},{6,7},{7,6},{8,9},{9,8},{10,11... | collective-permute-start | bytes 3538952 | tf_op jit(solution)/shard_map/ppermute | solution.py:247
  24.0 15.6 %collective-permute-start.1 = (bf16[128,4608]{1,0:T(8,128)(2,1)}, bf16[128,4608]{1,0:T(8,128)(2,1)S(1)}, u32[]{:S(2)}, u32[]{:S(2)}) collective-permute-start(bf16[128,4608]{1,0:T(8,128)(2,1)} %collective-permute-done.refs_0_), channel_id=1, source_target_pairs={{0,32},{1,225},{2,34},{3,227},{32,64},{33,1},{34,66},{35,3},{64,96... | collective-permute-start | bytes 3538952 | tf_op jit(solution)/shard_map/ppermute | solution.py:232
  31.9 29.7 %all-to-all-start = ((s16[8,800,128]{2,1,0:T(8,128)(2,1)}), s16[8,800,128]{2,1,0:T(8,128)(2,1)}, u32[]{:S(2)}, u32[]{:S(2)}) async-start(s16[8,800,128]{2,1,0:T(8,128)(2,1)} %grams.5), calls=%async_computation | async-start | bytes 3276800 | tf_op jit(solution)/shard_map/all_to_all | solution.py:254
  39.5 4.5 %collective-permute-start.5 = (bf16[128,4608]{1,0:T(8,128)(2,1)S(1)}, bf16[128,4608]{1,0:T(8,128)(2,1)S(1)}, u32[]{:S(2)}, u32[]{:S(2)}) collective-permute-start(bf16[128,4608]{1,0:T(8,128)(2,1)S(1)} %collective-permute-done.1.refs_0_), channel_id=1, source_target_pairs={{0,1},{1,0},{2,3},{3,2},{4,5},{5,4},{6,7},{7,6},{8,9},{9,8},{10,11... | collective-permute-start | bytes 3538952 | tf_op jit(solution)/shard_map/ppermute | solution.py:247
  41.7 9.4 %collective-permute-start.3 = (bf16[64,4608]{1,0:T(8,128)(2,1)S(1)}, bf16[64,4608]{1,0:T(8,128)(2,1)}, u32[]{:S(2)}, u32[]{:S(2)}) collective-permute-start(bf16[64,4608]{1,0:T(8,128)(2,1)S(1)} %get-tuple-element.15), channel_id=1, source_target_pairs={{0,32},{1,225},{2,34},{3,227},{32,64},{33,1},{34,66},{35,3},{64,96... | collective-permute-start | bytes 1769480 | tf_op jit(solution)/shard_map/ppermute | solution.py:232
  42.4 14.9 %collective-permute-start.4 = (bf16[64,4608]{1,0:T(8,128)(2,1)S(1)}, bf16[64,4608]{1,0:T(8,128)(2,1)}, u32[]{:S(2)}, u32[]{:S(2)}) collective-permute-start(bf16[64,4608]{1,0:T(8,128)(2,1)S(1)} %get-tuple-element.14), channel_id=1, source_target_pairs={{0,32},{1,225},{2,34},{3,227},{32,64},{33,1},{34,66},{35,3},{64,96... | collective-permute-start | bytes 1769480 | tf_op jit(solution)/shard_map/ppermute | solution.py:232
  44.1 3.1 %copy-start.2 = (bf16[1,1024,3584]{2,1,0:T(8,128)(2,1)S(1)}, bf16[1,1024,3584]{2,1,0:T(8,128)(2,1)}, u32[]{:S(2)}) copy-start(bf16[1,1024,3584]{2,1,0:T(8,128)(2,1)} %param.7) | copy-start | bytes 22020100
  57.2 9.8 %collective-permute-start.8 = (bf16[64,4608]{1,0:T(8,128)(2,1)}, bf16[64,4608]{1,0:T(8,128)(2,1)}, u32[]{:S(2)}, u32[]{:S(2)}) collective-permute-start(bf16[64,4608]{1,0:T(8,128)(2,1)} %collective-permute-done.3.refs_0_), channel_id=1, source_target_pairs={{0,32},{1,225},{2,34},{3,227},{32,64},{33,1},{34,66},{35,3},{64,96... | collective-permute-start | bytes 1769480 | tf_op jit(solution)/shard_map/ppermute | solution.py:232
  61.7 20.9 %all-to-all-start.1 = ((s16[8,528,128]{2,1,0:T(8,128)(2,1)}), s16[8,528,128]{2,1,0:T(8,128)(2,1)S(1)}, u32[]{:S(2)}, u32[]{:S(2)}) async-start(s16[8,528,128]{2,1,0:T(8,128)(2,1)} %grams.6), calls=%async_computation.1 | async-start | bytes 2162688 | tf_op jit(solution)/shard_map/all_to_all | solution.py:254
  65.5 5.2 %collective-permute-start.6 = (bf16[64,4608]{1,0:T(8,128)(2,1)}, bf16[64,4608]{1,0:T(8,128)(2,1)S(1)}, u32[]{:S(2)}, u32[]{:S(2)}) collective-permute-start(bf16[64,4608]{1,0:T(8,128)(2,1)} %collective-permute-done.3.refs_0_), channel_id=1, source_target_pairs={{0,1},{1,0},{2,3},{3,2},{4,5},{5,4},{6,7},{7,6},{8,9},{9,8},{10,11... | collective-permute-start | bytes 1769480 | tf_op jit(solution)/shard_map/ppermute | solution.py:247
  66.9 3.8 %collective-permute-start.7 = (bf16[64,4608]{1,0:T(8,128)(2,1)}, bf16[64,4608]{1,0:T(8,128)(2,1)S(1)}, u32[]{:S(2)}, u32[]{:S(2)}) collective-permute-start(bf16[64,4608]{1,0:T(8,128)(2,1)} %collective-permute-done.4.refs_1_), channel_id=1, source_target_pairs={{0,1},{1,0},{2,3},{3,2},{4,5},{5,4},{6,7},{7,6},{8,9},{9,8},{10,11... | collective-permute-start | bytes 1769480 | tf_op jit(solution)/shard_map/ppermute | solution.py:247
  67.0 5.6 %collective-permute-start.9 = (bf16[64,4608]{1,0:T(8,128)(2,1)}, bf16[64,4608]{1,0:T(8,128)(2,1)S(1)}, u32[]{:S(2)}, u32[]{:S(2)}) collective-permute-start(bf16[64,4608]{1,0:T(8,128)(2,1)} %collective-permute-done.8.refs_4_), channel_id=1, source_target_pairs={{0,1},{1,0},{2,3},{3,2},{4,5},{5,4},{6,7},{7,6},{8,9},{9,8},{10,11... | collective-permute-start | bytes 1769480 | tf_op jit(solution)/shard_map/ppermute | solution.py:247
  72.6 3.1 %copy-start.3 = (bf16[1,1024,3584]{2,1,0:T(8,128)(2,1)S(1)}, bf16[1,1024,3584]{2,1,0:T(8,128)(2,1)}, u32[]{:S(2)}) copy-start(bf16[1,1024,3584]{2,1,0:T(8,128)(2,1)} %param.7) | copy-start | bytes 22020100
  82.6 29.3 %all-to-all-start.2 = ((s16[8,784,128]{2,1,0:T(8,128)(2,1)}), s16[8,784,128]{2,1,0:T(8,128)(2,1)S(1)}, u32[]{:S(2)}, u32[]{:S(2)}) async-start(s16[8,784,128]{2,1,0:T(8,128)(2,1)} %grams.7), calls=%async_computation.2 | async-start | bytes 3211264 | tf_op jit(solution)/shard_map/all_to_all | solution.py:254
  113.0 12.1 %all-to-all-start.3 = ((f32[32,1,128]{2,1,0:T(1,128)}), f32[32,1,128]{2,1,0:T(1,128)S(1)}, u32[]{:S(2)}, u32[]{:S(2)}) async-start(f32[32,1,128]{2,1,0:T(1,128)} %bitcast.5), calls=%async_computation.3 | async-start | bytes 32768 | tf_op jit(solution)/shard_map/all_to_all | solution.py:262

commit v3 on v2

--- a/solution.py
+++ b/solution.py
@@ -79,6 +79,31 @@
         + [pltpu.SemaphoreType.DMA((3,))],
         8,
     )(core, *arrays)
+
+
+def load_kernel(source_ref, target_ref, sems):
+    rows = source_ref.shape[0] // sems.shape[0]
+    copies = []
+    for part in range(sems.shape[0]):
+        span = pl.ds(part * rows, rows)
+        source, target = source_ref.at[span, :], target_ref.at[span, :]
+        copies.append(pltpu.make_async_copy(source, target, sems.at[part]))
+    for copy in copies:
+        copy.start()
+    for copy in copies:
+        copy.wait()
+
+
+def load(array):
+    return kernel_call(
+        load_kernel,
+        "load",
+        pltpu.VMEM(array.shape, array.dtype),
+        [pl.BlockSpec(memory_space=pltpu.HBM)],
+        IN_VMEM,
+        4 * array.size,
+        [pltpu.SemaphoreType.DMA((4,))],
+    )(pltpu.with_memory_space_constraint(array, pltpu.HBM))
 
 
 def encode(gram):
@@ -245,6 +270,9 @@
         elif distance == last - 1:
             moving = pass_on(here[:1])
         waiting += here + [lax.ppermute(block, "seq", swap) for block in here]
+        if distance == last:
+            grad, _ = lax.optimization_barrier((train_grad, here[0]))
+            train = (train_act, load(grad))
         if distance == last - 1:
             continue
         counts, before = (sum(block.shape[0] for block in waiting),), ()

time: 126 us -> 125 us (level)
  Pallas kernels: 28.2 us -> 31.4 us
  local copies, waits for them, and re-layouts: 9.41 us -> 6.3 us
    pallas_call x0 -> x1, Pallas kernels: none -> 3.18 us  [load(): kernel_call(load_kernel, 'load', pltpu.VMEM(array.shape, array.dtype), [p...]
    unnamed x10 -> x8, local copies, waits for them, and re-layouts: 9.33 us -> 6.22 us
    ppermute x5, waiting for transfers between devices: 3.84 us -> 2.01 us  [per_device(): waiting += here + [lax.ppermute(block, 'seq', swap) for block in here]]
  transfers between devices with their start and end apart: 14 -> 14, of which waited for: 9 -> 9; matrix products, arithmetic and copies ran while one was open for 0% -> 0% of each run, Pallas kernels for 20% -> 23%
where the time goes in v3:
time: 125 us; the launch traced here: 124 us
  waiting for transfers between devices  43.1 us (34%)
  starting transfers between devices  41.8 us (33%)
  Pallas kernels  31.4 us (25%)
  local copies, waits for them, and re-layouts  6.3 us (5%)
  between operations  1.56 us (1%)
    all_to_all x3, waiting for transfers between devices, per_device(): sent.append((counts, lax.all_to_all(codes, 'tensor', 0, 0, tiled=True)))  24.2 us
    pallas_call x4, Pallas kernels, grams(): kernel_call(functools.partial(gram_kernel, len(blocks), len(before)), 'gr...  22.7 us
    all_to_all x3, starting transfers between devices, per_device(): sent.append((counts, lax.all_to_all(codes, 'tensor', 0, 0, tiled=True)))  16.5 us
    ppermute x5, starting transfers between devices, pass_on(): return [lax.ppermute(block, ('dp', 'seq'), along) for block in blocks]  11.4 us
    ppermute x5, waiting for transfers between devices, pass_on(): return [lax.ppermute(block, ('dp', 'seq'), along) for block in blocks]  10.5 us
    ppermute x5, starting transfers between devices, per_device(): waiting += here + [lax.ppermute(block, 'seq', swap) for block in here]  9.34 us
    all_to_all x1, waiting for transfers between devices, per_device(): everyone = lax.all_to_all(everyone, ('tensor', 'seq'), 0, 0, tiled=True)  6.4 us
    unnamed x8, local copies, waits for them, and re-layouts  6.22 us
  transfers between devices with their start and end apart: 14, of which 9 were waited for; matrix products, arithmetic and copies ran while one was open for 0% of the time, Pallas kernels for 23%

profile of v3, /device:TPU:1, one launch (start us, length us, event | category | flops | bytes accessed | tf_op | source)
XLA Modules:
  0.0 124.2 jit_solution(5677758568494731454)
XLA Ops:
  0.6 0.0 copy-start.3
  0.6 1.6 %prepare.1.refs_0_ = bf16[128,4608]{1,0:T(8,128)(2,1)S(1)} custom-call(s32[1]{0:T(128)S(6)} %and.4.core_ref, s32[1,128]{1,0:T(1,128)} %bitcast.17, bf16[128,1024]{1,0:T(8,128)(2,1)} %act_in.1, bf16[128,3584]{1,0:T(8,128)(2,1)} %grad_in.1), custom_call_target="tpu_custom_call" | custom-call | bytes 4718592 | tf_op jit(solution)/shard_map/prepare/pallas_call | solution.py:71
  2.3 6.5 %collective-permute-start = (bf16[128,4608]{1,0:T(8,128)(2,1)S(1)}, bf16[128,4608]{1,0:T(8,128)(2,1)}, u32[]{:S(2)}, u32[]{:S(2)}) collective-permute-start(bf16[128,4608]{1,0:T(8,128)(2,1)S(1)} %prepare.1.refs_0_), channel_id=1, source_target_pairs={{0,32},{1,225},{2,34},{3,227},{32,64},{33,1},{34,66},{35,3},{64,96... | collective-permute-start | bytes 3538952 | tf_op jit(solution)/shard_map/ppermute | solution.py:257
  8.7 0.0 copy-done.3
  8.7 0.0 copy-start
  8.7 3.1 %copy-done = bf16[1,1024,3584]{2,1,0:T(8,128)(2,1)S(1)} copy-done((bf16[1,1024,3584]{2,1,0:T(8,128)(2,1)S(1)}, bf16[1,1024,3584]{2,1,0:T(8,128)(2,1)}, u32[]{:S(2)}) %copy-start) | copy-done | bytes 7340056
  11.9 0.0 copy-start.1
  11.9 6.6 %grams.4.refs_2_ = s16[8,272,128]{2,1,0:T(8,128)(2,1)S(1)} custom-call(bf16[1024,1024]{1,0:T(8,128)(2,1)S(1)} %bitcast.12, bf16[1024,3584]{1,0:T(8,128)(2,1)S(1)} %bitcast.9, bf16[128,4608]{1,0:T(8,128)(2,1)S(1)} %prepare.1.refs_0_), custom_call_target="tpu_custom_call" | custom-call | bytes 524288 | tf_op jit(solution)/shard_map/grams/pallas_call | solution.py:156
  18.4 3.5 %collective-permute-done.refs_0_ = bf16[128,4608]{1,0:T(8,128)(2,1)} collective-permute-done((bf16[128,4608]{1,0:T(8,128)(2,1)S(1)}, bf16[128,4608]{1,0:T(8,128)(2,1)}, u32[]{:S(2)}, u32[]{:S(2)}) %collective-permute-start) | collective-permute-done | bytes 1179680 | tf_op jit(solution)/shard_map/ppermute | solution.py:257
  21.9 2.1 %collective-permute-start.2 = (bf16[128,4608]{1,0:T(8,128)(2,1)}, bf16[128,4608]{1,0:T(8,128)(2,1)S(1)}, u32[]{:S(2)}, u32[]{:S(2)}) collective-permute-start(bf16[128,4608]{1,0:T(8,128)(2,1)} %collective-permute-done.refs_0_), channel_id=1, source_target_pairs={{0,1},{1,0},{2,3},{3,2},{4,5},{5,4},{6,7},{7,6},{8,9},{9,8},{10,11... | collective-permute-start | bytes 3538952 | tf_op jit(solution)/shard_map/ppermute | solution.py:272
  24.0 1.7 %collective-permute-start.1 = (bf16[128,4608]{1,0:T(8,128)(2,1)}, bf16[128,4608]{1,0:T(8,128)(2,1)S(1)}, u32[]{:S(2)}, u32[]{:S(2)}) collective-permute-start(bf16[128,4608]{1,0:T(8,128)(2,1)} %collective-permute-done.refs_0_), channel_id=1, source_target_pairs={{0,32},{1,225},{2,34},{3,227},{32,64},{33,1},{34,66},{35,3},{64,96... | collective-permute-start | bytes 3538952 | tf_op jit(solution)/shard_map/ppermute | solution.py:257
  25.7 0.9 collective-permute-done.2.refs_1_
  26.7 0.0 copy-done.1
  26.7 5.3 %grams.5 = s16[8,800,128]{2,1,0:T(8,128)(2,1)} custom-call(bf16[1024,1024]{1,0:T(8,128)(2,1)S(1)} %bitcast.13, bf16[1024,3584]{1,0:T(8,128)(2,1)S(1)} %bitcast.10, bf16[128,4608]{1,0:T(8,128)(2,1)} %collective-permute-done.refs_0_, bf16[128,4608]{1,0:T(8,128)(2,1)S(1)} %collective-permute-done.2.refs_1_, s16[8,272,128]{2,1,0:T(8,128)(2,1)S(1)} %grams.4.refs_2_), custom_call_target="tpu_custom_call" | custom-call | bytes 1048576 | tf_op jit(solution)/shard_map/grams/pallas_call | solution.py:156
  31.9 6.7 %all-to-all-start = ((s16[8,800,128]{2,1,0:T(8,128)(2,1)}), s16[8,800,128]{2,1,0:T(8,128)(2,1)}, u32[]{:S(2)}, u32[]{:S(2)}) async-start(s16[8,800,128]{2,1,0:T(8,128)(2,1)} %grams.5), calls=%async_computation | async-start | bytes 3276800 | tf_op jit(solution)/shard_map/all_to_all | solution.py:282
  38.6 0.9 collective-permute-done.1.refs_0_
  39.5 2.1 %collective-permute-start.5 = (bf16[128,4608]{1,0:T(8,128)(2,1)S(1)}, bf16[128,4608]{1,0:T(8,128)(2,1)S(1)}, u32[]{:S(2)}, u32[]{:S(2)}) collective-permute-start(bf16[128,4608]{1,0:T(8,128)(2,1)S(1)} %collective-permute-done.1.refs_0_), channel_id=1, source_target_pairs={{0,1},{1,0},{2,3},{3,2},{4,5},{5,4},{6,7},{7,6},{8,9},{9,8},{10,11... | collective-permute-start | bytes 3538952 | tf_op jit(solution)/shard_map/ppermute | solution.py:272
  41.6 0.1 fusion
  41.7 0.7 collective-permute-start.3
  42.4 0.7 collective-permute-start.4
  43.0 1.1 collective-permute-done.5.refs_1_
  44.1 0.0 copy-start.2
  44.1 3.1 %copy-done.2 = bf16[1,1024,3584]{2,1,0:T(8,128)(2,1)S(1)} copy-done((bf16[1,1024,3584]{2,1,0:T(8,128)(2,1)S(1)}, bf16[1,1024,3584]{2,1,0:T(8,128)(2,1)}, u32[]{:S(2)}) %copy-start.2) | copy-done | bytes 7340056
  47.2 3.9 %grams.6 = s16[8,528,128]{2,1,0:T(8,128)(2,1)} custom-call(bf16[1024,1024]{1,0:T(8,128)(2,1)S(1)} %bitcast.14, bf16[1024,3584]{1,0:T(8,128)(2,1)S(1)} %bitcast.11, bf16[128,4608]{1,0:T(8,128)(2,1)S(1)} %collective-permute-done.1.refs_0_, bf16[128,4608]{1,0:T(8,128)(2,1)S(1)} %collective-permute-done.5.refs_1_), custom_call_target="tpu_custom_call" | custom-call | bytes 1048576 | tf_op jit(solution)/shard_map/grams/pallas_call | solution.py:156
  51.1 0.0 collective-permute-done.3.refs_0_
  51.1 6.1 %collective-permute-done.4.refs_1_ = bf16[64,4608]{1,0:T(8,128)(2,1)} collective-permute-done((bf16[64,4608]{1,0:T(8,128)(2,1)S(1)}, bf16[64,4608]{1,0:T(8,128)(2,1)}, u32[]{:S(2)}, u32[]{:S(2)}) %collective-permute-start.4) | collective-permute-done | bytes 589856 | tf_op jit(solution)/shard_map/ppermute | solution.py:257
  57.2 1.8 %collective-permute-start.6 = (bf16[64,4608]{1,0:T(8,128)(2,1)}, bf16[64,4608]{1,0:T(8,128)(2,1)}, u32[]{:S(2)}, u32[]{:S(2)}) collective-permute-start(bf16[64,4608]{1,0:T(8,128)(2,1)} %collective-permute-done.3.refs_0_), channel_id=1, source_target_pairs={{0,32},{1,225},{2,34},{3,227},{32,64},{33,1},{34,66},{35,3},{64,96... | collective-permute-start | bytes 1769480 | tf_op jit(solution)/shard_map/ppermute | solution.py:257
  59.0 2.6 %all-to-all-done.piece_ref = s16[8,800,128]{2,1,0:T(8,128)(2,1)} async-done(((s16[8,800,128]{2,1,0:T(8,128)(2,1)}), s16[8,800,128]{2,1,0:T(8,128)(2,1)}, u32[]{:S(2)}, u32[]{:S(2)}) %all-to-all-start) | async-done | bytes 1638432 | tf_op jit(solution)/shard_map/all_to_all | solution.py:282
  61.7 3.9 %all-to-all-start.1 = ((s16[8,528,128]{2,1,0:T(8,128)(2,1)}), s16[8,528,128]{2,1,0:T(8,128)(2,1)S(1)}, u32[]{:S(2)}, u32[]{:S(2)}) async-start(s16[8,528,128]{2,1,0:T(8,128)(2,1)} %grams.6), calls=%async_computation.1 | async-start | bytes 2162688 | tf_op jit(solution)/shard_map/all_to_all | solution.py:282
  65.5 1.4 %collective-permute-start.7 = (bf16[64,4608]{1,0:T(8,128)(2,1)}, bf16[64,4608]{1,0:T(8,128)(2,1)S(1)}, u32[]{:S(2)}, u32[]{:S(2)}) collective-permute-start(bf16[64,4608]{1,0:T(8,128)(2,1)} %collective-permute-done.3.refs_0_), channel_id=1, source_target_pairs={{0,1},{1,0},{2,3},{3,2},{4,5},{5,4},{6,7},{7,6},{8,9},{9,8},{10,11... | collective-permute-start | bytes 1769480 | tf_op jit(solution)/shard_map/ppermute | solution.py:272
  66.9 0.1 collective-permute-start.8
  67.0 0.0 collective-permute-done.6.refs_4_
  67.0 3.7 %collective-permute-start.9 = (bf16[64,4608]{1,0:T(8,128)(2,1)}, bf16[64,4608]{1,0:T(8,128)(2,1)S(1)}, u32[]{:S(2)}, u32[]{:S(2)}) collective-permute-start(bf16[64,4608]{1,0:T(8,128)(2,1)} %collective-permute-done.6.refs_4_), channel_id=1, source_target_pairs={{0,1},{1,0},{2,3},{3,2},{4,5},{5,4},{6,7},{7,6},{8,9},{9,8},{10,11... | collective-permute-start | bytes 1769480 | tf_op jit(solution)/shard_map/ppermute | solution.py:272
  70.7 3.2 %load.1.grad_ref = bf16[1024,3584]{1,0:T(8,128)(2,1)S(1)} custom-call(bf16[1024,3584]{1,0:T(8,128)(2,1)} %bitcast.8), custom_call_target="tpu_custom_call" | custom-call | bytes 14680064 | tf_op jit(solution)/shard_map/load/pallas_call | solution.py:98
  73.9 0.0 collective-permute-done.7.refs_2_
  73.9 0.0 collective-permute-done.8.refs_3_
  73.9 0.0 collective-permute-done.9.refs_5_
  73.9 7.0 %grams.7 = s16[8,784,128]{2,1,0:T(8,128)(2,1)} custom-call(bf16[1024,1024]{1,0:T(8,128)(2,1)S(1)} %bitcast.15, bf16[1024,3584]{1,0:T(8,128)(2,1)S(1)} %load.1.grad_ref, bf16[64,4608]{1,0:T(8,128)(2,1)} %collective-permute-done.3.refs_0_, bf16[64,4608]{1,0:T(8,128)(2,1)} %collective-permute-done.4.refs_1_, ...), custom_call_target="tpu_custom_call" | custom-call | bytes 1572864 | tf_op jit(solution)/shard_map/grams/pallas_call | solution.py:156
  80.9 0.7 all-to-all-done.1.piece_ref
  81.6 6.0 %all-to-all-start.2 = ((s16[8,784,128]{2,1,0:T(8,128)(2,1)}), s16[8,784,128]{2,1,0:T(8,128)(2,1)S(1)}, u32[]{:S(2)}, u32[]{:S(2)}) async-start(s16[8,784,128]{2,1,0:T(8,128)(2,1)} %grams.7), calls=%async_computation.2 | async-start | bytes 3211264 | tf_op jit(solution)/shard_map/all_to_all | solution.py:282
  87.6 1.9 %reduce.3.before_ref = f32[1,128]{1,0:T(1,128)S(1)} custom-call(f32[1,128]{1,0:T(1,128)S(1)} %broadcast_in_dim.3.before_ref, s16[8,800,128]{2,1,0:T(8,128)(2,1)} %all-to-all-done.piece_ref), custom_call_target="tpu_custom_call" | custom-call | bytes 1638400 | tf_op jit(solution)/shard_map/reduce/pallas_call | solution.py:195
  89.5 0.3 reduce.4.before_ref
  89.8 20.8 %all-to-all-done.2.piece_ref = s16[8,784,128]{2,1,0:T(8,128)(2,1)S(1)} async-done(((s16[8,784,128]{2,1,0:T(8,128)(2,1)}), s16[8,784,128]{2,1,0:T(8,128)(2,1)S(1)}, u32[]{:S(2)}, u32[]{:S(2)}) %all-to-all-start.2) | async-done | bytes 1605664 | tf_op jit(solution)/shard_map/all_to_all | solution.py:282
  110.6 1.1 reduce.5
  111.7 4.6 %all-to-all-start.3 = ((f32[32,1,128]{2,1,0:T(1,128)}), f32[32,1,128]{2,1,0:T(1,128)S(1)}, u32[]{:S(2)}, u32[]{:S(2)}) async-start(f32[32,1,128]{2,1,0:T(1,128)} %bitcast.5), calls=%async_computation.3 | async-start | bytes 32768 | tf_op jit(solution)/shard_map/all_to_all | solution.py:290
  117.0 6.4 %all-to-all-done.3 = f32[32,1,128]{2,1,0:T(1,128)S(1)} async-done(((f32[32,1,128]{2,1,0:T(1,128)}), f32[32,1,128]{2,1,0:T(1,128)S(1)}, u32[]{:S(2)}, u32[]{:S(2)}) %all-to-all-start.3) | async-done | bytes 16416 | tf_op jit(solution)/shard_map/all_to_all | solution.py:290
  123.4 0.6 finish.1
  (1 shorter events, 0.0 us)
Async XLA Ops:
  0.6 8.1 %copy-start.3 = (bf16[1,1024,1024]{2,1,0:T(8,128)(2,1)S(1)}, bf16[1,1024,1024]{2,1,0:T(8,128)(2,1)}, u32[]{:S(2)}) copy-start(bf16[1,1024,1024]{2,1,0:T(8,128)(2,1)} %param.6) | copy-start | bytes 6291460
  2.3 19.6 %collective-permute-start = (bf16[128,4608]{1,0:T(8,128)(2,1)S(1)}, bf16[128,4608]{1,0:T(8,128)(2,1)}, u32[]{:S(2)}, u32[]{:S(2)}) collective-permute-start(bf16[128,4608]{1,0:T(8,128)(2,1)S(1)} %prepare.1.refs_0_), channel_id=1, source_target_pairs={{0,32},{1,225},{2,34},{3,227},{32,64},{33,1},{34,66},{35,3},{64,96... | collective-permute-start | bytes 3538952 | tf_op jit(solution)/shard_map/ppermute | solution.py:257
  8.7 3.1 %copy-start = (bf16[1,1024,3584]{2,1,0:T(8,128)(2,1)S(1)}, bf16[1,1024,3584]{2,1,0:T(8,128)(2,1)}, u32[]{:S(2)}) copy-start(bf16[1,1024,3584]{2,1,0:T(8,128)(2,1)} %param.7) | copy-start | bytes 22020100
  11.9 14.8 %copy-start.1 = (bf16[1,1024,3584]{2,1,0:T(8,128)(2,1)S(1)}, bf16[1,1024,3584]{2,1,0:T(8,128)(2,1)}, u32[]{:S(2)}) copy-start(bf16[1,1024,3584]{2,1,0:T(8,128)(2,1)} %param.7) | copy-start | bytes 22020100
  21.9 4.8 %collective-permute-start.2 = (bf16[128,4608]{1,0:T(8,128)(2,1)}, bf16[128,4608]{1,0:T(8,128)(2,1)S(1)}, u32[]{:S(2)}, u32[]{:S(2)}) collective-permute-start(bf16[128,4608]{1,0:T(8,128)(2,1)} %collective-permute-done.refs_0_), channel_id=1, source_target_pairs={{0,1},{1,0},{2,3},{3,2},{4,5},{5,4},{6,7},{7,6},{8,9},{9,8},{10,11... | collective-permute-start | bytes 3538952 | tf_op jit(solution)/shard_map/ppermute | solution.py:272
  24.0 15.6 %collective-permute-start.1 = (bf16[128,4608]{1,0:T(8,128)(2,1)}, bf16[128,4608]{1,0:T(8,128)(2,1)S(1)}, u32[]{:S(2)}, u32[]{:S(2)}) collective-permute-start(bf16[128,4608]{1,0:T(8,128)(2,1)} %collective-permute-done.refs_0_), channel_id=1, source_target_pairs={{0,32},{1,225},{2,34},{3,227},{32,64},{33,1},{34,66},{35,3},{64,96... | collective-permute-start | bytes 3538952 | tf_op jit(solution)/shard_map/ppermute | solution.py:257
  31.9 29.7 %all-to-all-start = ((s16[8,800,128]{2,1,0:T(8,128)(2,1)}), s16[8,800,128]{2,1,0:T(8,128)(2,1)}, u32[]{:S(2)}, u32[]{:S(2)}) async-start(s16[8,800,128]{2,1,0:T(8,128)(2,1)} %grams.5), calls=%async_computation | async-start | bytes 3276800 | tf_op jit(solution)/shard_map/all_to_all | solution.py:282
  39.5 4.5 %collective-permute-start.5 = (bf16[128,4608]{1,0:T(8,128)(2,1)S(1)}, bf16[128,4608]{1,0:T(8,128)(2,1)S(1)}, u32[]{:S(2)}, u32[]{:S(2)}) collective-permute-start(bf16[128,4608]{1,0:T(8,128)(2,1)S(1)} %collective-permute-done.1.refs_0_), channel_id=1, source_target_pairs={{0,1},{1,0},{2,3},{3,2},{4,5},{5,4},{6,7},{7,6},{8,9},{9,8},{10,11... | collective-permute-start | bytes 3538952 | tf_op jit(solution)/shard_map/ppermute | solution.py:272
  41.7 9.4 %collective-permute-start.3 = (bf16[64,4608]{1,0:T(8,128)(2,1)S(1)}, bf16[64,4608]{1,0:T(8,128)(2,1)}, u32[]{:S(2)}, u32[]{:S(2)}) collective-permute-start(bf16[64,4608]{1,0:T(8,128)(2,1)S(1)} %get-tuple-element.17), channel_id=1, source_target_pairs={{0,32},{1,225},{2,34},{3,227},{32,64},{33,1},{34,66},{35,3},{64,96... | collective-permute-start | bytes 1769480 | tf_op jit(solution)/shard_map/ppermute | solution.py:257
  42.4 14.9 %collective-permute-start.4 = (bf16[64,4608]{1,0:T(8,128)(2,1)S(1)}, bf16[64,4608]{1,0:T(8,128)(2,1)}, u32[]{:S(2)}, u32[]{:S(2)}) collective-permute-start(bf16[64,4608]{1,0:T(8,128)(2,1)S(1)} %get-tuple-element.16), channel_id=1, source_target_pairs={{0,32},{1,225},{2,34},{3,227},{32,64},{33,1},{34,66},{35,3},{64,96... | collective-permute-start | bytes 1769480 | tf_op jit(solution)/shard_map/ppermute | solution.py:257
  44.1 3.1 %copy-start.2 = (bf16[1,1024,3584]{2,1,0:T(8,128)(2,1)S(1)}, bf16[1,1024,3584]{2,1,0:T(8,128)(2,1)}, u32[]{:S(2)}) copy-start(bf16[1,1024,3584]{2,1,0:T(8,128)(2,1)} %param.7) | copy-start | bytes 22020100
  57.2 9.8 %collective-permute-start.6 = (bf16[64,4608]{1,0:T(8,128)(2,1)}, bf16[64,4608]{1,0:T(8,128)(2,1)}, u32[]{:S(2)}, u32[]{:S(2)}) collective-permute-start(bf16[64,4608]{1,0:T(8,128)(2,1)} %collective-permute-done.3.refs_0_), channel_id=1, source_target_pairs={{0,32},{1,225},{2,34},{3,227},{32,64},{33,1},{34,66},{35,3},{64,96... | collective-permute-start | bytes 1769480 | tf_op jit(solution)/shard_map/ppermute | solution.py:257
  61.7 19.9 %all-to-all-start.1 = ((s16[8,528,128]{2,1,0:T(8,128)(2,1)}), s16[8,528,128]{2,1,0:T(8,128)(2,1)S(1)}, u32[]{:S(2)}, u32[]{:S(2)}) async-start(s16[8,528,128]{2,1,0:T(8,128)(2,1)} %grams.6), calls=%async_computation.1 | async-start | bytes 2162688 | tf_op jit(solution)/shard_map/all_to_all | solution.py:282
  65.5 8.4 %collective-permute-start.7 = (bf16[64,4608]{1,0:T(8,128)(2,1)}, bf16[64,4608]{1,0:T(8,128)(2,1)S(1)}, u32[]{:S(2)}, u32[]{:S(2)}) collective-permute-start(bf16[64,4608]{1,0:T(8,128)(2,1)} %collective-permute-done.3.refs_0_), channel_id=1, source_target_pairs={{0,1},{1,0},{2,3},{3,2},{4,5},{5,4},{6,7},{7,6},{8,9},{9,8},{10,11... | collective-permute-start | bytes 1769480 | tf_op jit(solution)/shard_map/ppermute | solution.py:272
  66.9 7.0 %collective-permute-start.8 = (bf16[64,4608]{1,0:T(8,128)(2,1)}, bf16[64,4608]{1,0:T(8,128)(2,1)S(1)}, u32[]{:S(2)}, u32[]{:S(2)}) collective-permute-start(bf16[64,4608]{1,0:T(8,128)(2,1)} %collective-permute-done.4.refs_1_), channel_id=1, source_target_pairs={{0,1},{1,0},{2,3},{3,2},{4,5},{5,4},{6,7},{7,6},{8,9},{9,8},{10,11... | collective-permute-start | bytes 1769480 | tf_op jit(solution)/shard_map/ppermute | solution.py:272
  67.0 6.9 %collective-permute-start.9 = (bf16[64,4608]{1,0:T(8,128)(2,1)}, bf16[64,4608]{1,0:T(8,128)(2,1)S(1)}, u32[]{:S(2)}, u32[]{:S(2)}) collective-permute-start(bf16[64,4608]{1,0:T(8,128)(2,1)} %collective-permute-done.6.refs_4_), channel_id=1, source_target_pairs={{0,1},{1,0},{2,3},{3,2},{4,5},{5,4},{6,7},{7,6},{8,9},{9,8},{10,11... | collective-permute-start | bytes 1769480 | tf_op jit(solution)/shard_map/ppermute | solution.py:272
  81.6 29.0 %all-to-all-start.2 = ((s16[8,784,128]{2,1,0:T(8,128)(2,1)}), s16[8,784,128]{2,1,0:T(8,128)(2,1)S(1)}, u32[]{:S(2)}, u32[]{:S(2)}) async-start(s16[8,784,128]{2,1,0:T(8,128)(2,1)} %grams.7), calls=%async_computation.2 | async-start | bytes 3211264 | tf_op jit(solution)/shard_map/all_to_all | solution.py:282
  111.7 11.7 %all-to-all-start.3 = ((f32[32,1,128]{2,1,0:T(1,128)}), f32[32,1,128]{2,1,0:T(1,128)S(1)}, u32[]{:S(2)}, u32[]{:S(2)}) async-start(f32[32,1,128]{2,1,0:T(1,128)} %bitcast.5), calls=%async_computation.3 | async-start | bytes 32768 | tf_op jit(solution)/shard_map/all_to_all | solution.py:290

commit v4 on v3

--- a/solution.py
+++ b/solution.py
@@ -18,7 +18,7 @@
 
 
 def kernel_call(
-    kernel, name, out_shape, in_specs, out_specs, moved, scratch=(), grant=4
+    kernel, name, out_shape, in_specs, out_specs, moved, scratch=(), grant=4, aliases=None
 ):
     return pl.pallas_call(
         kernel,
@@ -27,6 +27,7 @@
         in_specs=in_specs,
         out_specs=out_specs,
         scratch_shapes=scratch,
+        input_output_aliases=aliases or {},
         compiler_params=pltpu.CompilerParams(vmem_limit_bytes=grant * 2**20),
         cost_estimate=pl.CostEstimate(flops=0, bytes_accessed=moved, transcendentals=0),
     )
@@ -113,9 +114,8 @@
     return codes.astype(jnp.int32).astype(jnp.int16), step.astype(jnp.int32)
 
 
-def gram_kernel(n_blocks, n_before, act_ref, grad_ref, *refs):
-    block_refs, refs = refs[:n_blocks], refs[n_blocks:]
-    before_refs, (out_ref, val_ref, code_ref, sems) = refs[:n_before], refs[n_before:]
+def gram_kernel(n_blocks, first, act_ref, grad_ref, *refs):
+    block_refs, (out_ref, val_ref, code_ref, sems) = refs[:n_blocks], refs[-4:]
     start = 0
     for ref in block_refs:
         val_ref[start : start + ref.shape[0], :] = ref[...]
@@ -123,8 +123,7 @@
     count = val_ref.shape[0]
     tokens, width = act_ref.shape
     each = TILE // LANES
-    for ref in before_refs:
-        code_ref[:, 2 * count + EXTRA :, :] = ref[...]
+    span = pl.ds(first, 2 * count + EXTRA)
     copies = []
     for tile in range(tokens // TILE):
         rows = slice(tile * TILE, (tile + 1) * TILE)
@@ -140,25 +139,29 @@
             code_ref[peer, 2 * count : 2 * count + EXTRA, :] = steps[:, lanes]
         peers = pl.ds(tile * each, each)
         copies.append(
-            pltpu.make_async_copy(code_ref.at[peers], out_ref.at[peers], sems.at[tile])
+            pltpu.make_async_copy(
+                code_ref.at[peers], out_ref.at[peers, span, :], sems.at[tile]
+            )
         )
         copies[-1].start()
     for copy in copies:
         copy.wait()
 
 
-def grams(train, blocks, before=(), place=pltpu.HBM):
+def grams(train, blocks, first=0, shared=()):
     tokens = train[0].shape[0]
     width = train[0].shape[1] + train[1].shape[1]
     count = sum(block.shape[0] for block in blocks)
-    rows = 2 * count + EXTRA + sum(codes.shape[1] for codes in before)
+    rows = 2 * count + EXTRA
     shape = (tokens // LANES, rows, LANES)
-    return kernel_call(
-        functools.partial(gram_kernel, len(blocks), len(before)),
+    in_hbm = pl.BlockSpec(memory_space=pltpu.HBM)
+    whole = shared[0].shape if shared else (shape[0], first + rows, LANES)
+    return kernel_call(
+        functools.partial(gram_kernel, len(blocks), first),
         "grams",
-        place(shape, jnp.int16),
-        [IN_VMEM] * (2 + len(blocks) + len(before)),
-        pl.BlockSpec(memory_space=place),
+        pltpu.HBM(whole, jnp.int16),
+        [IN_VMEM] * (2 + len(blocks)) + [in_hbm] * len(shared),
+        in_hbm,
         4 * tokens * count,
         [
             pltpu.VMEM((count, width), jnp.bfloat16),
@@ -166,7 +169,8 @@
             pltpu.SemaphoreType.DMA((tokens // TILE,)),
         ],
         12,
-    )(*train, *blocks, *before)
+        {2 + len(blocks): 0} if shared else None,
+    )(*train, *blocks, *shared)
 
 
 def reduce_kernel(counts, scale, before_ref, piece_ref, out_ref):
@@ -259,10 +263,12 @@
     train = (train_act, train_grad)
     last = ring // 2
     moving = pass_on(own)
-    codes = grams(train, own, (), pltpu.VMEM)
-    own_codes, waiting, sent = codes, [], []
+    codes = grams(train, own, 4 * val_rows + EXTRA)
+    waiting, sent = [], []
     for distance in range(1, last + 1):
-        here, codes, own_codes = lax.optimization_barrier((moving, codes, own_codes))
+        here, codes = lax.optimization_barrier((moving, codes))
+        if distance == 1:
+            own_codes = codes
         if distance < last - 2:
             moving = pass_on(here)
         elif distance == last - 2:
@@ -275,10 +281,10 @@
             train = (train_act, load(grad))
         if distance == last - 1:
             continue
-        counts, before = (sum(block.shape[0] for block in waiting),), ()
+        counts, shared = (sum(block.shape[0] for block in waiting),), ()
         if distance == 1:
-            counts, before = counts + (val_rows,), (own_codes,)
-        codes, waiting = grams(train, waiting, before), []
+            counts, shared = counts + (val_rows,), (own_codes,)
+        codes, waiting = grams(train, waiting, 0, shared), []
         sent.append((counts, lax.all_to_all(codes, "tensor", 0, 0, tiled=True)))
     values = jnp.zeros((1, LANES), jnp.float32)
     values, codes = lax.optimization_barrier((values, codes))

time: 125 us -> 125 us (level)
  waiting for transfers between devices: 43.1 us -> 46.8 us
  Pallas kernels: 31.4 us -> 28.7 us
    ppermute x5, waiting for transfers between devices: 10.5 us -> 13.3 us  [pass_on(): return [lax.ppermute(block, ('dp', 'seq'), along) for block in blocks]]
    pallas_call x4, Pallas kernels: 22.7 us -> 19.9 us  [grams(): kernel_call(functools.partial(gram_kernel, len(blocks), first), 'grams',...]
  transfers between devices with their start and end apart: 14 -> 14, of which waited for: 9 -> 9; matrix products, arithmetic and copies ran while one was open for 0% -> 0% of each run, Pallas kernels for 23% -> 20%
where the time goes in v4:
time: 125 us; the launch traced here: 124 us
  waiting for transfers between devices  46.8 us (37%)
  starting transfers between devices  40.8 us (33%)
  Pallas kernels  28.7 us (23%)
  local copies, waits for them, and re-layouts  6.3 us (5%)
  between operations  1.56 us (1%)
    all_to_all x3, waiting for transfers between devices, per_device(): sent.append((counts, lax.all_to_all(codes, 'tensor', 0, 0, tiled=True)))  25.1 us
    pallas_call x4, Pallas kernels, grams(): kernel_call(functools.partial(gram_kernel, len(blocks), first), 'grams',...  19.9 us
    all_to_all x3, starting transfers between devices, per_device(): sent.append((counts, lax.all_to_all(codes, 'tensor', 0, 0, tiled=True)))  15.8 us
    ppermute x5, waiting for transfers between devices, pass_on(): return [lax.ppermute(block, ('dp', 'seq'), along) for block in blocks]  13.3 us
    ppermute x5, starting transfers between devices, pass_on(): return [lax.ppermute(block, ('dp', 'seq'), along) for block in blocks]  11.4 us
    ppermute x5, starting transfers between devices, per_device(): waiting += here + [lax.ppermute(block, 'seq', swap) for block in here]  8.96 us
    all_to_all x1, waiting for transfers between devices, per_device(): everyone = lax.all_to_all(everyone, ('tensor', 'seq'), 0, 0, tiled=True)  6.4 us
    unnamed x8, local copies, waits for them, and re-layouts  6.22 us
  transfers between devices with their start and end apart: 14, of which 9 were waited for; matrix products, arithmetic and copies ran while one was open for 0% of the time, Pallas kernels for 20%

profile of v4, /device:TPU:1, one launch (start us, length us, event | category | flops | bytes accessed | tf_op | source)
XLA Modules:
  0.0 124.2 jit_solution(4126551414642996052)
XLA Ops:
  0.6 0.0 copy-start.3
  0.6 1.6 %prepare.1.refs_0_ = bf16[128,4608]{1,0:T(8,128)(2,1)S(1)} custom-call(s32[1]{0:T(128)S(6)} %and.4.core_ref, s32[1,128]{1,0:T(1,128)} %bitcast.17, bf16[128,1024]{1,0:T(8,128)(2,1)} %act_in.1, bf16[128,3584]{1,0:T(8,128)(2,1)} %grad_in.1), custom_call_target="tpu_custom_call" | custom-call | bytes 4718592 | tf_op jit(solution)/shard_map/prepare/pallas_call | solution.py:72
  2.3 6.5 %collective-permute-start = (bf16[128,4608]{1,0:T(8,128)(2,1)S(1)}, bf16[128,4608]{1,0:T(8,128)(2,1)}, u32[]{:S(2)}, u32[]{:S(2)}) collective-permute-start(bf16[128,4608]{1,0:T(8,128)(2,1)S(1)} %prepare.1.refs_0_), channel_id=1, source_target_pairs={{0,32},{1,225},{2,34},{3,227},{32,64},{33,1},{34,66},{35,3},{64,96... | collective-permute-start | bytes 3538952 | tf_op jit(solution)/shard_map/ppermute | solution.py:261
  8.7 0.0 copy-done.3
  8.7 0.0 copy-start
  8.7 3.1 %copy-done = bf16[1,1024,3584]{2,1,0:T(8,128)(2,1)S(1)} copy-done((bf16[1,1024,3584]{2,1,0:T(8,128)(2,1)S(1)}, bf16[1,1024,3584]{2,1,0:T(8,128)(2,1)}, u32[]{:S(2)}) %copy-start) | copy-done | bytes 7340056
  11.9 0.0 copy-start.1
  11.9 3.9 %grams.4.refs_2_ = s16[8,800,128]{2,1,0:T(8,128)(2,1)} custom-call(bf16[1024,1024]{1,0:T(8,128)(2,1)S(1)} %bitcast.12, bf16[1024,3584]{1,0:T(8,128)(2,1)S(1)} %bitcast.9, bf16[128,4608]{1,0:T(8,128)(2,1)S(1)} %prepare.1.refs_0_), custom_call_target="tpu_custom_call" | custom-call | bytes 524288 | tf_op jit(solution)/shard_map/grams/pallas_call | solution.py:159
  15.8 6.1 %collective-permute-done.refs_0_ = bf16[128,4608]{1,0:T(8,128)(2,1)} collective-permute-done((bf16[128,4608]{1,0:T(8,128)(2,1)S(1)}, bf16[128,4608]{1,0:T(8,128)(2,1)}, u32[]{:S(2)}, u32[]{:S(2)}) %collective-permute-start) | collective-permute-done | bytes 1179680 | tf_op jit(solution)/shard_map/ppermute | solution.py:261
  21.9 2.1 %collective-permute-start.2 = (bf16[128,4608]{1,0:T(8,128)(2,1)}, bf16[128,4608]{1,0:T(8,128)(2,1)S(1)}, u32[]{:S(2)}, u32[]{:S(2)}) collective-permute-start(bf16[128,4608]{1,0:T(8,128)(2,1)} %collective-permute-done.refs_0_), channel_id=1, source_target_pairs={{0,1},{1,0},{2,3},{3,2},{4,5},{5,4},{6,7},{7,6},{8,9},{9,8},{10,11... | collective-permute-start | bytes 3538952 | tf_op jit(solution)/shard_map/ppermute | solution.py:278
  24.0 1.7 %collective-permute-start.1 = (bf16[128,4608]{1,0:T(8,128)(2,1)}, bf16[128,4608]{1,0:T(8,128)(2,1)S(1)}, u32[]{:S(2)}, u32[]{:S(2)}) collective-permute-start(bf16[128,4608]{1,0:T(8,128)(2,1)} %collective-permute-done.refs_0_), channel_id=1, source_target_pairs={{0,32},{1,225},{2,34},{3,227},{32,64},{33,1},{34,66},{35,3},{64,96... | collective-permute-start | bytes 3538952 | tf_op jit(solution)/shard_map/ppermute | solution.py:261
  25.7 0.9 collective-permute-done.2.refs_1_
  26.7 0.0 copy-done.1
  26.7 5.1 %grams.5 = s16[8,800,128]{2,1,0:T(8,128)(2,1)} custom-call(bf16[1024,1024]{1,0:T(8,128)(2,1)S(1)} %bitcast.13, bf16[1024,3584]{1,0:T(8,128)(2,1)S(1)} %bitcast.10, bf16[128,4608]{1,0:T(8,128)(2,1)} %collective-permute-done.refs_0_, bf16[128,4608]{1,0:T(8,128)(2,1)S(1)} %collective-permute-done.2.refs_1_, ...), custom_call_target="tpu_custom_call", output_to_operand_aliasing={{}: (4, {})} | custom-call | bytes 1048576 | tf_op jit(solution)/shard_map/grams/pallas_call | solution.py:159
  31.8 6.7 %all-to-all-start = ((s16[8,800,128]{2,1,0:T(8,128)(2,1)}), s16[8,800,128]{2,1,0:T(8,128)(2,1)}, u32[]{:S(2)}, u32[]{:S(2)}) async-start(s16[8,800,128]{2,1,0:T(8,128)(2,1)} %grams.5), calls=%async_computation | async-start | bytes 3276800 | tf_op jit(solution)/shard_map/all_to_all | solution.py:288
  38.5 1.1 collective-permute-done.1.refs_0_
  39.5 2.1 %collective-permute-start.5 = (bf16[128,4608]{1,0:T(8,128)(2,1)S(1)}, bf16[128,4608]{1,0:T(8,128)(2,1)S(1)}, u32[]{:S(2)}, u32[]{:S(2)}) collective-permute-start(bf16[128,4608]{1,0:T(8,128)(2,1)S(1)} %collective-permute-done.1.refs_0_), channel_id=1, source_target_pairs={{0,1},{1,0},{2,3},{3,2},{4,5},{5,4},{6,7},{7,6},{8,9},{9,8},{10,11... | collective-permute-start | bytes 3538952 | tf_op jit(solution)/shard_map/ppermute | solution.py:278
  41.6 0.1 fusion
  41.7 0.7 collective-permute-start.3
  42.4 0.7 collective-permute-start.4
  43.0 1.1 collective-permute-done.5.refs_1_
  44.1 0.0 copy-start.2
  44.1 3.1 %copy-done.2 = bf16[1,1024,3584]{2,1,0:T(8,128)(2,1)S(1)} copy-done((bf16[1,1024,3584]{2,1,0:T(8,128)(2,1)S(1)}, bf16[1,1024,3584]{2,1,0:T(8,128)(2,1)}, u32[]{:S(2)}) %copy-start.2) | copy-done | bytes 7340056
  47.2 3.9 %grams.6 = s16[8,528,128]{2,1,0:T(8,128)(2,1)} custom-call(bf16[1024,1024]{1,0:T(8,128)(2,1)S(1)} %bitcast.14, bf16[1024,3584]{1,0:T(8,128)(2,1)S(1)} %bitcast.11, bf16[128,4608]{1,0:T(8,128)(2,1)S(1)} %collective-permute-done.1.refs_0_, bf16[128,4608]{1,0:T(8,128)(2,1)S(1)} %collective-permute-done.5.refs_1_), custom_call_target="tpu_custom_call" | custom-call | bytes 1048576 | tf_op jit(solution)/shard_map/grams/pallas_call | solution.py:159
  51.1 0.0 collective-permute-done.3.refs_0_
  51.1 6.1 %collective-permute-done.4.refs_1_ = bf16[64,4608]{1,0:T(8,128)(2,1)} collective-permute-done((bf16[64,4608]{1,0:T(8,128)(2,1)S(1)}, bf16[64,4608]{1,0:T(8,128)(2,1)}, u32[]{:S(2)}, u32[]{:S(2)}) %collective-permute-start.4) | collective-permute-done | bytes 589856 | tf_op jit(solution)/shard_map/ppermute | solution.py:261
  57.2 1.8 %collective-permute-start.6 = (bf16[64,4608]{1,0:T(8,128)(2,1)}, bf16[64,4608]{1,0:T(8,128)(2,1)}, u32[]{:S(2)}, u32[]{:S(2)}) collective-permute-start(bf16[64,4608]{1,0:T(8,128)(2,1)} %collective-permute-done.3.refs_0_), channel_id=1, source_target_pairs={{0,32},{1,225},{2,34},{3,227},{32,64},{33,1},{34,66},{35,3},{64,96... | collective-permute-start | bytes 1769480 | tf_op jit(solution)/shard_map/ppermute | solution.py:261
  59.0 2.5 %all-to-all-done.piece_ref = s16[8,800,128]{2,1,0:T(8,128)(2,1)} async-done(((s16[8,800,128]{2,1,0:T(8,128)(2,1)}), s16[8,800,128]{2,1,0:T(8,128)(2,1)}, u32[]{:S(2)}, u32[]{:S(2)}) %all-to-all-start) | async-done | bytes 1638432 | tf_op jit(solution)/shard_map/all_to_all | solution.py:288
  61.5 4.4 %all-to-all-start.1 = ((s16[8,528,128]{2,1,0:T(8,128)(2,1)}), s16[8,528,128]{2,1,0:T(8,128)(2,1)S(1)}, u32[]{:S(2)}, u32[]{:S(2)}) async-start(s16[8,528,128]{2,1,0:T(8,128)(2,1)} %grams.6), calls=%async_computation.1 | async-start | bytes 2162688 | tf_op jit(solution)/shard_map/all_to_all | solution.py:288
  65.9 1.0 collective-permute-start.7
  66.9 0.1 collective-permute-start.8
  67.0 0.0 collective-permute-done.6.refs_4_
  67.0 3.7 %collective-permute-start.9 = (bf16[64,4608]{1,0:T(8,128)(2,1)}, bf16[64,4608]{1,0:T(8,128)(2,1)S(1)}, u32[]{:S(2)}, u32[]{:S(2)}) collective-permute-start(bf16[64,4608]{1,0:T(8,128)(2,1)} %collective-permute-done.6.refs_4_), channel_id=1, source_target_pairs={{0,1},{1,0},{2,3},{3,2},{4,5},{5,4},{6,7},{7,6},{8,9},{9,8},{10,11... | collective-permute-start | bytes 1769480 | tf_op jit(solution)/shard_map/ppermute | solution.py:278
  70.7 3.2 %load.1.grad_ref = bf16[1024,3584]{1,0:T(8,128)(2,1)S(1)} custom-call(bf16[1024,3584]{1,0:T(8,128)(2,1)} %bitcast.8), custom_call_target="tpu_custom_call" | custom-call | bytes 14680064 | tf_op jit(solution)/shard_map/load/pallas_call | solution.py:99
  73.9 0.0 collective-permute-done.7.refs_2_
  73.9 0.0 collective-permute-done.8.refs_3_
  73.9 0.0 collective-permute-done.9.refs_5_
  73.9 7.0 %grams.7 = s16[8,784,128]{2,1,0:T(8,128)(2,1)} custom-call(bf16[1024,1024]{1,0:T(8,128)(2,1)S(1)} %bitcast.15, bf16[1024,3584]{1,0:T(8,128)(2,1)S(1)} %load.1.grad_ref, bf16[64,4608]{1,0:T(8,128)(2,1)} %collective-permute-done.3.refs_0_, bf16[64,4608]{1,0:T(8,128)(2,1)} %collective-permute-done.4.refs_1_, ...), custom_call_target="tpu_custom_call" | custom-call | bytes 1572864 | tf_op jit(solution)/shard_map/grams/pallas_call | solution.py:159
  80.9 1.9 %all-to-all-done.1.piece_ref = s16[8,528,128]{2,1,0:T(8,128)(2,1)S(1)} async-done(((s16[8,528,128]{2,1,0:T(8,128)(2,1)}), s16[8,528,128]{2,1,0:T(8,128)(2,1)S(1)}, u32[]{:S(2)}, u32[]{:S(2)}) %all-to-all-start.1) | async-done | bytes 1081376 | tf_op jit(solution)/shard_map/all_to_all | solution.py:288
  82.8 4.8 %all-to-all-start.2 = ((s16[8,784,128]{2,1,0:T(8,128)(2,1)}), s16[8,784,128]{2,1,0:T(8,128)(2,1)S(1)}, u32[]{:S(2)}, u32[]{:S(2)}) async-start(s16[8,784,128]{2,1,0:T(8,128)(2,1)} %grams.7), calls=%async_computation.2 | async-start | bytes 3211264 | tf_op jit(solution)/shard_map/all_to_all | solution.py:288
  87.6 1.9 %reduce.3.before_ref = f32[1,128]{1,0:T(1,128)S(1)} custom-call(f32[1,128]{1,0:T(1,128)S(1)} %broadcast_in_dim.3.before_ref, s16[8,800,128]{2,1,0:T(8,128)(2,1)} %all-to-all-done.piece_ref), custom_call_target="tpu_custom_call" | custom-call | bytes 1638400 | tf_op jit(solution)/shard_map/reduce/pallas_call | solution.py:199
  89.5 0.3 reduce.4.before_ref
  89.8 20.7 %all-to-all-done.2.piece_ref = s16[8,784,128]{2,1,0:T(8,128)(2,1)S(1)} async-done(((s16[8,784,128]{2,1,0:T(8,128)(2,1)}), s16[8,784,128]{2,1,0:T(8,128)(2,1)S(1)}, u32[]{:S(2)}, u32[]{:S(2)}) %all-to-all-start.2) | async-done | bytes 1605664 | tf_op jit(solution)/shard_map/all_to_all | solution.py:288
  110.5 1.1 reduce.5
  111.6 4.7 %all-to-all-start.3 = ((f32[32,1,128]{2,1,0:T(1,128)}), f32[32,1,128]{2,1,0:T(1,128)S(1)}, u32[]{:S(2)}, u32[]{:S(2)}) async-start(f32[32,1,128]{2,1,0:T(1,128)} %bitcast.5), calls=%async_computation.3 | async-start | bytes 32768 | tf_op jit(solution)/shard_map/all_to_all | solution.py:296
  117.0 6.4 %all-to-all-done.3 = f32[32,1,128]{2,1,0:T(1,128)S(1)} async-done(((f32[32,1,128]{2,1,0:T(1,128)}), f32[32,1,128]{2,1,0:T(1,128)S(1)}, u32[]{:S(2)}, u32[]{:S(2)}) %all-to-all-start.3) | async-done | bytes 16416 | tf_op jit(solution)/shard_map/all_to_all | solution.py:296
  123.4 0.6 finish.1
  (1 shorter events, 0.0 us)
Async XLA Ops:
  0.6 8.1 %copy-start.3 = (bf16[1,1024,1024]{2,1,0:T(8,128)(2,1)S(1)}, bf16[1,1024,1024]{2,1,0:T(8,128)(2,1)}, u32[]{:S(2)}) copy-start(bf16[1,1024,1024]{2,1,0:T(8,128)(2,1)} %param.6) | copy-start | bytes 6291460
  2.3 19.6 %collective-permute-start = (bf16[128,4608]{1,0:T(8,128)(2,1)S(1)}, bf16[128,4608]{1,0:T(8,128)(2,1)}, u32[]{:S(2)}, u32[]{:S(2)}) collective-permute-start(bf16[128,4608]{1,0:T(8,128)(2,1)S(1)} %prepare.1.refs_0_), channel_id=1, source_target_pairs={{0,32},{1,225},{2,34},{3,227},{32,64},{33,1},{34,66},{35,3},{64,96... | collective-permute-start | bytes 3538952 | tf_op jit(solution)/shard_map/ppermute | solution.py:261
  8.7 3.1 %copy-start = (bf16[1,1024,3584]{2,1,0:T(8,128)(2,1)S(1)}, bf16[1,1024,3584]{2,1,0:T(8,128)(2,1)}, u32[]{:S(2)}) copy-start(bf16[1,1024,3584]{2,1,0:T(8,128)(2,1)} %param.7) | copy-start | bytes 22020100
  11.9 14.8 %copy-start.1 = (bf16[1,1024,3584]{2,1,0:T(8,128)(2,1)S(1)}, bf16[1,1024,3584]{2,1,0:T(8,128)(2,1)}, u32[]{:S(2)}) copy-start(bf16[1,1024,3584]{2,1,0:T(8,128)(2,1)} %param.7) | copy-start | bytes 22020100
  21.9 4.8 %collective-permute-start.2 = (bf16[128,4608]{1,0:T(8,128)(2,1)}, bf16[128,4608]{1,0:T(8,128)(2,1)S(1)}, u32[]{:S(2)}, u32[]{:S(2)}) collective-permute-start(bf16[128,4608]{1,0:T(8,128)(2,1)} %collective-permute-done.refs_0_), channel_id=1, source_target_pairs={{0,1},{1,0},{2,3},{3,2},{4,5},{5,4},{6,7},{7,6},{8,9},{9,8},{10,11... | collective-permute-start | bytes 3538952 | tf_op jit(solution)/shard_map/ppermute | solution.py:278
  24.0 15.6 %collective-permute-start.1 = (bf16[128,4608]{1,0:T(8,128)(2,1)}, bf16[128,4608]{1,0:T(8,128)(2,1)S(1)}, u32[]{:S(2)}, u32[]{:S(2)}) collective-permute-start(bf16[128,4608]{1,0:T(8,128)(2,1)} %collective-permute-done.refs_0_), channel_id=1, source_target_pairs={{0,32},{1,225},{2,34},{3,227},{32,64},{33,1},{34,66},{35,3},{64,96... | collective-permute-start | bytes 3538952 | tf_op jit(solution)/shard_map/ppermute | solution.py:261
  31.8 29.7 %all-to-all-start = ((s16[8,800,128]{2,1,0:T(8,128)(2,1)}), s16[8,800,128]{2,1,0:T(8,128)(2,1)}, u32[]{:S(2)}, u32[]{:S(2)}) async-start(s16[8,800,128]{2,1,0:T(8,128)(2,1)} %grams.5), calls=%async_computation | async-start | bytes 3276800 | tf_op jit(solution)/shard_map/all_to_all | solution.py:288
  39.5 4.5 %collective-permute-start.5 = (bf16[128,4608]{1,0:T(8,128)(2,1)S(1)}, bf16[128,4608]{1,0:T(8,128)(2,1)S(1)}, u32[]{:S(2)}, u32[]{:S(2)}) collective-permute-start(bf16[128,4608]{1,0:T(8,128)(2,1)S(1)} %collective-permute-done.1.refs_0_), channel_id=1, source_target_pairs={{0,1},{1,0},{2,3},{3,2},{4,5},{5,4},{6,7},{7,6},{8,9},{9,8},{10,11... | collective-permute-start | bytes 3538952 | tf_op jit(solution)/shard_map/ppermute | solution.py:278
  41.7 9.4 %collective-permute-start.3 = (bf16[64,4608]{1,0:T(8,128)(2,1)S(1)}, bf16[64,4608]{1,0:T(8,128)(2,1)}, u32[]{:S(2)}, u32[]{:S(2)}) collective-permute-start(bf16[64,4608]{1,0:T(8,128)(2,1)S(1)} %get-tuple-element.17), channel_id=1, source_target_pairs={{0,32},{1,225},{2,34},{3,227},{32,64},{33,1},{34,66},{35,3},{64,96... | collective-permute-start | bytes 1769480 | tf_op jit(solution)/shard_map/ppermute | solution.py:261
  42.4 14.9 %collective-permute-start.4 = (bf16[64,4608]{1,0:T(8,128)(2,1)S(1)}, bf16[64,4608]{1,0:T(8,128)(2,1)}, u32[]{:S(2)}, u32[]{:S(2)}) collective-permute-start(bf16[64,4608]{1,0:T(8,128)(2,1)S(1)} %get-tuple-element.16), channel_id=1, source_target_pairs={{0,32},{1,225},{2,34},{3,227},{32,64},{33,1},{34,66},{35,3},{64,96... | collective-permute-start | bytes 1769480 | tf_op jit(solution)/shard_map/ppermute | solution.py:261
  44.1 3.1 %copy-start.2 = (bf16[1,1024,3584]{2,1,0:T(8,128)(2,1)S(1)}, bf16[1,1024,3584]{2,1,0:T(8,128)(2,1)}, u32[]{:S(2)}) copy-start(bf16[1,1024,3584]{2,1,0:T(8,128)(2,1)} %param.7) | copy-start | bytes 22020100
  57.2 9.8 %collective-permute-start.6 = (bf16[64,4608]{1,0:T(8,128)(2,1)}, bf16[64,4608]{1,0:T(8,128)(2,1)}, u32[]{:S(2)}, u32[]{:S(2)}) collective-permute-start(bf16[64,4608]{1,0:T(8,128)(2,1)} %collective-permute-done.3.refs_0_), channel_id=1, source_target_pairs={{0,32},{1,225},{2,34},{3,227},{32,64},{33,1},{34,66},{35,3},{64,96... | collective-permute-start | bytes 1769480 | tf_op jit(solution)/shard_map/ppermute | solution.py:261
  61.5 21.3 %all-to-all-start.1 = ((s16[8,528,128]{2,1,0:T(8,128)(2,1)}), s16[8,528,128]{2,1,0:T(8,128)(2,1)S(1)}, u32[]{:S(2)}, u32[]{:S(2)}) async-start(s16[8,528,128]{2,1,0:T(8,128)(2,1)} %grams.6), calls=%async_computation.1 | async-start | bytes 2162688 | tf_op jit(solution)/shard_map/all_to_all | solution.py:288
  65.9 8.0 %collective-permute-start.7 = (bf16[64,4608]{1,0:T(8,128)(2,1)}, bf16[64,4608]{1,0:T(8,128)(2,1)S(1)}, u32[]{:S(2)}, u32[]{:S(2)}) collective-permute-start(bf16[64,4608]{1,0:T(8,128)(2,1)} %collective-permute-done.3.refs_0_), channel_id=1, source_target_pairs={{0,1},{1,0},{2,3},{3,2},{4,5},{5,4},{6,7},{7,6},{8,9},{9,8},{10,11... | collective-permute-start | bytes 1769480 | tf_op jit(solution)/shard_map/ppermute | solution.py:278
  66.9 7.0 %collective-permute-start.8 = (bf16[64,4608]{1,0:T(8,128)(2,1)}, bf16[64,4608]{1,0:T(8,128)(2,1)S(1)}, u32[]{:S(2)}, u32[]{:S(2)}) collective-permute-start(bf16[64,4608]{1,0:T(8,128)(2,1)} %collective-permute-done.4.refs_1_), channel_id=1, source_target_pairs={{0,1},{1,0},{2,3},{3,2},{4,5},{5,4},{6,7},{7,6},{8,9},{9,8},{10,11... | collective-permute-start | bytes 1769480 | tf_op jit(solution)/shard_map/ppermute | solution.py:278
  67.0 6.9 %collective-permute-start.9 = (bf16[64,4608]{1,0:T(8,128)(2,1)}, bf16[64,4608]{1,0:T(8,128)(2,1)S(1)}, u32[]{:S(2)}, u32[]{:S(2)}) collective-permute-start(bf16[64,4608]{1,0:T(8,128)(2,1)} %collective-permute-done.6.refs_4_), channel_id=1, source_target_pairs={{0,1},{1,0},{2,3},{3,2},{4,5},{5,4},{6,7},{7,6},{8,9},{9,8},{10,11... | collective-permute-start | bytes 1769480 | tf_op jit(solution)/shard_map/ppermute | solution.py:278
  82.8 27.7 %all-to-all-start.2 = ((s16[8,784,128]{2,1,0:T(8,128)(2,1)}), s16[8,784,128]{2,1,0:T(8,128)(2,1)S(1)}, u32[]{:S(2)}, u32[]{:S(2)}) async-start(s16[8,784,128]{2,1,0:T(8,128)(2,1)} %grams.7), calls=%async_computation.2 | async-start | bytes 3211264 | tf_op jit(solution)/shard_map/all_to_all | solution.py:288
  111.6 11.8 %all-to-all-start.3 = ((f32[32,1,128]{2,1,0:T(1,128)}), f32[32,1,128]{2,1,0:T(1,128)S(1)}, u32[]{:S(2)}, u32[]{:S(2)}) async-start(f32[32,1,128]{2,1,0:T(1,128)} %bitcast.5), calls=%async_computation.3 | async-start | bytes 32768 | tf_op jit(solution)/shard_map/all_to_all | solution.py:296
